TPU v7x, 512 devices: a whole 4x8x8 slice. The times are simulated.
512 devices in a mesh: freq: 8 (over z), trow: 4 (over x), tcol: 16 (over y, core).
Axes of the slice: x: 4, y: 8, z: 8, core: 2. Of those that a mesh axis runs over, the one named last changes fastest.
Arguments:
- traces: bfloat16 [16, 16, 1024, 1024], P('freq', 'tcol', 'trow'), may hold values from -6 to 6
- u_bases: bfloat16 [8, 32, 64, 2, 32, 256], P('freq', 'trow', 'tcol'), may hold values from -0.09375 to 0.09375
- v_bases: bfloat16 [8, 32, 64, 2, 32, 256], P('freq', 'trow', 'tcol'), may hold values from -0.25 to 0.25
- ranks: int32 [8, 32, 64], P('freq', 'trow', 'tcol'), may hold values from 1 to 32, as said below
- observed: float32 [8, 2, 16, 8192], P('freq', None, None, 'trow'), may hold values from -6 to 6
Outputs:
- residual: float32 [8, 2, 16, 8192], P('freq', None, None, 'trow')
- gradient: bfloat16 [16, 16, 1024, 1024], P('freq', 'tcol', 'trow')
Inputs may be any that keep to these rules, and one draw needn't show every extreme that they name: `ranks`: each tile's rank at each frequency; at every frequency some tile has rank 32.
All inputs are finite; a program needn't handle non-finite values.
Results may differ from a plain program's by a relative error of at most 0.023.
Values may be sent and summed in bfloat16 or wider, within the bound.
No kernel may reach another device: no remote copies, remote signals or barrier semaphores. Data moves between devices by JAX's collectives and lax.ppermute only.
A program may use at most 64 MiB of HBM per device.

v0:
```python
import math

import jax
import jax.numpy as jnp
from jax import lax
from jax.sharding import PartitionSpec as P

FIRST_BIN = 40


def dft_table(freq_count, first_bin, trace_len):
    freq_bins = first_bin + jnp.arange(freq_count, dtype=jnp.int32)
    time_steps = jnp.arange(trace_len, dtype=jnp.int32)
    phase_index = freq_bins[:, None] * time_steps[None, :] % trace_len
    angles = phase_index.astype(jnp.float32) * (2.0 * math.pi / trace_len)
    return jnp.stack([jnp.cos(angles), -jnp.sin(angles)], axis=1).astype(jnp.bfloat16)


def conj_project(basis_set, operand, einsum_form):
    swapped = jnp.stack([operand[:, 1], -operand[:, 0]], axis=1)
    real_component = jnp.einsum(einsum_form, basis_set, operand, preferred_element_type=jnp.float32)
    imag_part = jnp.einsum(einsum_form, basis_set, swapped, preferred_element_type=jnp.float32)
    return (real_component, imag_part)


def apply_ranks(real_component, imag_part, ranks, cap_used):
    rank_mask_array = (
        jnp.arange(cap_used, dtype=jnp.int32)[None, None, None, :] < ranks[..., None]
    ).astype(jnp.float32)[..., None]
    return (
        (real_component * rank_mask_array).astype(jnp.bfloat16),
        (imag_part * rank_mask_array).astype(jnp.bfloat16),
    )


def expand_terms(basis_set, real_component, imag_part, einsum_form):
    first_coef = jnp.stack([real_component, -imag_part], axis=3)
    second_coef = jnp.stack([imag_part, real_component], axis=3)
    return jnp.stack(
        [
            jnp.einsum(einsum_form, basis_set, first_coef, preferred_element_type=jnp.float32),
            jnp.einsum(einsum_form, basis_set, second_coef, preferred_element_type=jnp.float32),
        ],
        axis=1,
    )


def shards(traces, u_bases, v_bases, ranks, observed):
    local_freq = u_bases.shape[0]
    tiles_row = u_bases.shape[1]
    tiles_col = u_bases.shape[2]
    rank_cap = u_bases.shape[4]
    tile_len = u_bases.shape[5]
    virtual_source = observed.shape[2]
    freq_count = local_freq * lax.axis_size("freq")
    trace_len = traces.shape[3]
    basis_lookup_table = dft_table(freq_count, FIRST_BIN, trace_len)
    resident_traces = traces.reshape(traces.shape[0], traces.shape[2], trace_len)
    spectrum = (
        jnp.einsum(
            "gzq,odq->gzod", basis_lookup_table, resident_traces, preferred_element_type=jnp.float32
        )
        * (1.0 / math.sqrt(trace_len))
    ).astype(jnp.bfloat16)
    spectrum = lax.all_to_all(spectrum, "freq", split_axis=0, concat_axis=2, tiled=True)
    spectrum = lax.all_gather(spectrum, "trow", axis=3, tiled=True)
    column_entries = spectrum.reshape(local_freq, 2, virtual_source, tiles_col, tile_len)
    real_component, imag_part = conj_project(v_bases, column_entries, "fabckj,fcvbj->fabkv")
    real_component, imag_part = apply_ranks(real_component, imag_part, ranks, rank_cap)
    row_terms = expand_terms(u_bases, real_component, imag_part, "fabcki,fabckv->fvai")
    row_terms = row_terms.reshape(local_freq, 2, virtual_source, tiles_row * tile_len)
    row_grand_total = lax.psum(row_terms.astype(jnp.bfloat16), "tcol").astype(jnp.float32)
    residual = observed - row_grand_total
    row_data = residual.astype(jnp.bfloat16).reshape(
        local_freq, 2, virtual_source, tiles_row, tile_len
    )
    real_component, imag_part = conj_project(u_bases, row_data, "fabcki,fcvai->fabkv")
    real_component, imag_part = apply_ranks(real_component, imag_part, ranks, rank_cap)
    back_terms = expand_terms(v_bases, real_component, imag_part, "fabckj,fabckv->fvbj")
    back_terms = back_terms.reshape(local_freq, 2, virtual_source, tiles_col * tile_len)
    col_total = lax.psum(back_terms.astype(jnp.bfloat16), "trow").astype(jnp.float32)
    sub_len = back_terms.shape[3] // lax.axis_size("trow")
    summed = lax.dynamic_slice_in_dim(col_total, lax.axis_index("trow") * sub_len, sub_len, 3)
    packed = summed.astype(jnp.bfloat16)
    values = jnp.einsum(
        "nuz,nuhr->hrz",
        basis_lookup_table,
        lax.all_to_all(packed, "freq", split_axis=2, concat_axis=0, tiled=True),
        preferred_element_type=jnp.float32,
    )
    result = (values * (1.0 / math.sqrt(freq_count))).astype(jnp.bfloat16)
    gradient = result.reshape(result.shape[0], 1, result.shape[1], trace_len)
    return (residual, gradient)


def solution(mesh):
    placed = (
        P("freq", "tcol", "trow", None),
        P("freq", "trow", "tcol", None, None, None),
        P("freq", "trow", "tcol", None, None, None),
        P("freq", "trow", "tcol"),
        P("freq", None, None, "trow"),
    )
    return jax.shard_map(
        shards,
        mesh=mesh,
        in_specs=placed,
        out_specs=(P("freq", None, None, "trow"), P("freq", "tcol", "trow", None)),
        check_vma=False,
    )
```

profile of v0, /device:TPU:1, one launch (start us, length us, event | category | flops | bytes accessed | tf_op | source)
XLA Modules:
  0.0 227.4 jit_solution(3063349872583190835)
XLA Ops:
  7.2 0.0 copy-start
  7.2 0.0 copy-start.2
  7.2 0.0 copy-start.3
  7.2 0.2 cosine_convert_fusion
  7.4 1.8 fusion.20
  9.2 0.6 copy.43
  9.8 10.9 %all-to-all-start = ((bf16[8,2,2,256]{3,2,1,0:T(2,128)(2,1)}), bf16[8,2,2,256]{3,2,1,0:T(2,128)(2,1)S(1)}, u32[]{:S(2)}, u32[]{:S(2)}) async-start(bf16[8,2,2,256]{3,2,1,0:T(2,128)(2,1)} %copy.43), calls=%async_computation | async-start | bytes 32768 | tf_op jit(solution)/shard_map/all_to_all | solution.py:65
  20.7 0.0 all-reduce.3.cloned.1.call-start
  20.7 0.0 copy-done.2
  20.8 0.1 fusion.49
  20.8 6.5 %all-to-all-done = bf16[8,2,2,256]{3,2,1,0:T(2,128)(2,1)S(1)} async-done(((bf16[8,2,2,256]{3,2,1,0:T(2,128)(2,1)}), bf16[8,2,2,256]{3,2,1,0:T(2,128)(2,1)S(1)}, u32[]{:S(2)}, u32[]{:S(2)}) %all-to-all-start) | async-done | bytes 16416 | tf_op jit(solution)/shard_map/all_to_all | solution.py:65
  27.3 8.0 %all_gather.3 = bf16[1,2,16,1024]{3,1,2,0:T(2,128)(2,1)S(1)} all-gather(bf16[1,2,16,256]{3,1,2,0:T(2,128)(2,1)S(1)} %bitcast.209), channel_id=1, replica_groups=mesh['freq'=8,'trow'=4,'tcol'=16] {'trow'}, dimensions={3}, use_global_device_ids=true | all-gather | bytes 81920 | tf_op jit(solution)/shard_map/all_gather | solution.py:66
  35.6 0.0 copy-done.3
  35.6 0.8 fusion.11
  36.3 0.8 fusion.6
  37.2 0.1 maximum_bitcast_fusion
  37.3 0.0 copy-done
  37.3 0.3 fusion.15
  37.7 0.0 copy-start.1
  37.7 0.3 fusion.14
  38.2 0.7 pad_maximum_fusion
  38.8 0.0 all-reduce.3.cloned.1.call-update
  38.8 0.0 all-reduce.5.cloned.1.call-start
  38.9 110.5 %all-reduce.3.cloned.1.call-done = bf16[1,2,16,2048]{3,2,1,0:T(8,128)(2,1)} async-done(((bf16[1,2,16,2048]{3,2,1,0:T(8,128)(2,1)}), bf16[1,2,16,2048]{3,2,1,0:T(8,128)(2,1)}) %all-reduce.3.cloned.1.call-update) | async-done | bytes 131088 | tf_op jit(solution)/shard_map/psum | solution.py:72
  149.4 0.0 copy-done.1
  149.4 1.6 fusion.56
  151.2 0.8 fusion.10
  152.0 0.8 fusion.9
  152.8 0.1 maximum_bitcast_fusion.2
  152.9 0.3 fusion.19
  153.2 0.3 fusion.18
  153.7 0.6 pad_maximum_fusion.1
  154.3 0.0 all-reduce.5.cloned.1.call-update
  154.4 50.5 %all-reduce.5.cloned.1.call-done = bf16[1,2,16,1024]{3,2,1,0:T(8,128)(2,1)} async-done(((bf16[1,2,16,1024]{3,2,1,0:T(8,128)(2,1)}), bf16[1,2,16,1024]{3,2,1,0:T(8,128)(2,1)}) %all-reduce.5.cloned.1.call-update) | async-done | bytes 65552 | tf_op jit(solution)/shard_map/psum | solution.py:81
  204.9 0.7 convert_convert_fusion
  205.6 13.5 %all_to_all.36 = bf16[1,2,16,256]{3,1,0,2:T(2,128)(2,1)S(1)} all-to-all(bf16[1,2,16,256]{3,1,0,2:T(2,128)(2,1)S(1)} %copy.68), channel_id=1, replica_groups=mesh['freq'=8,'trow'=4,'tcol'=16] {'freq'}, dimensions={2} | all-to-all | bytes 32768 | tf_op jit(solution)/shard_map/all_to_all | solution.py:88
  219.1 1.4 fusion.1
  (24 shorter events, 0.5 us)
Async XLA Ops:
  7.2 30.1 %copy-start = (bf16[1,8,4,2,32,256]{5,4,3,2,1,0:T(8,128)(2,1)S(1)}, bf16[1,8,4,2,32,256]{5,4,3,2,1,0:T(8,128)(2,1)}, u32[]{:S(2)}) copy-start(bf16[1,8,4,2,32,256]{5,4,3,2,1,0:T(8,128)(2,1)} %param.6) | copy-start | bytes 3145732
  7.2 13.6 %copy-start.2 = (s32[1,8,4]{1,2,0:T(4,128)S(1)}, s32[1,8,4]{1,2,0:T(4,128)}, u32[]{:S(2)}) copy-start(s32[1,8,4]{1,2,0:T(4,128)} %param.8) | copy-start | bytes 388
  7.2 28.4 %copy-start.3 = (bf16[1,8,4,2,32,256]{5,4,3,2,1,0:T(8,128)(2,1)S(1)}, bf16[1,8,4,2,32,256]{5,4,3,2,1,0:T(8,128)(2,1)}, u32[]{:S(2)}) copy-start(bf16[1,8,4,2,32,256]{5,4,3,2,1,0:T(8,128)(2,1)} %param.7) | copy-start | bytes 3145732
  9.8 17.5 %all-to-all-start = ((bf16[8,2,2,256]{3,2,1,0:T(2,128)(2,1)}), bf16[8,2,2,256]{3,2,1,0:T(2,128)(2,1)S(1)}, u32[]{:S(2)}, u32[]{:S(2)}) async-start(bf16[8,2,2,256]{3,2,1,0:T(2,128)(2,1)} %copy.43), calls=%async_computation | async-start | bytes 32768 | tf_op jit(solution)/shard_map/all_to_all | solution.py:65
  20.7 128.7 %all-reduce.3.cloned.1.call-start = ((), (), s32[]{:S(2)}) async-start(), calls=%async_computation.2 | async-start | bytes 262144 | tf_op jit(solution)/shard_map/psum | solution.py:72
  37.7 111.7 %copy-start.1 = (f32[1,2,16,2048]{3,2,1,0:T(8,128)S(1)}, f32[1,2,16,2048]{3,2,1,0:T(8,128)}, u32[]{:S(2)}) copy-start(f32[1,2,16,2048]{3,2,1,0:T(8,128)} %param.9) | copy-start | bytes 786436
  38.8 166.0 %all-reduce.5.cloned.1.call-start = ((), (), s32[]{:S(2)}) async-start(), calls=%async_computation.3 | async-start | bytes 131072 | tf_op jit(solution)/shard_map/psum | solution.py:81
Sparse Core Ops, SparseCore 0:
  39.0 110.4 all-reduce.2
  154.5 50.3 all-reduce.4
where the time goes:
time: 230 us; the launch traced here: 227 us
  waiting for transfers between devices  168 us (73%)
  blocking collectives  21.6 us (9%)
  between operations  14.3 us (6%)
  starting transfers between devices  10.9 us (5%)
  matrix products  7.68 us (3%)
  other arithmetic  4.28 us (2%)
    psum x1, waiting for transfers between devices, shards(): lax.psum(row_terms.astype(jnp.bfloat16), 'tcol').astype(jnp.float32)  111 us
    psum x1, waiting for transfers between devices, shards(): lax.psum(back_terms.astype(jnp.bfloat16), 'trow').astype(jnp.float32)  50.5 us
    all_to_all x1, blocking collectives, shards(): lax.all_to_all(packed, 'freq', split_axis=2, concat_axis=0, tiled=True)  13.5 us
    all_to_all x1, starting transfers between devices, shards(): lax.all_to_all(spectrum, 'freq', split_axis=0, concat_axis=2, tiled=True)  10.9 us
    all_gather x1, blocking collectives, shards(): spectrum = lax.all_gather(spectrum, 'trow', axis=3, tiled=True)  8.05 us
    all_to_all x1, waiting for transfers between devices, shards(): lax.all_to_all(spectrum, 'freq', split_axis=0, concat_axis=2, tiled=True)  6.5 us
  transfers between devices with their start and end apart: 3, of which 3 were waited for; matrix products, arithmetic and copies ran while one was open for 0% of the time, Pallas kernels for 0%

commit v1 on v0

--- a/solution.py
+++ b/solution.py
@@ -62,14 +62,39 @@
         )
         * (1.0 / math.sqrt(trace_len))
     ).astype(jnp.bfloat16)
-    spectrum = lax.all_to_all(spectrum, "freq", split_axis=0, concat_axis=2, tiled=True)
-    spectrum = lax.all_gather(spectrum, "trow", axis=3, tiled=True)
-    column_entries = spectrum.reshape(local_freq, 2, virtual_source, tiles_col, tile_len)
+    row_shards = lax.axis_size("trow")
+    col_shards = lax.axis_size("tcol")
+    spectrum = jnp.broadcast_to(spectrum[:, None], (freq_count, row_shards) + spectrum.shape[1:])
+    spectrum = lax.all_to_all(
+        spectrum.reshape((freq_count * row_shards,) + spectrum.shape[2:]),
+        ("freq", "trow"),
+        split_axis=0,
+        concat_axis=0,
+        tiled=True,
+    )
+    spectrum = spectrum.reshape((freq_count, row_shards) + spectrum.shape[1:])
+    column_entries = spectrum.transpose(2, 0, 3, 1, 4).reshape(
+        local_freq, 2, virtual_source, tiles_col, tile_len
+    )
     real_component, imag_part = conj_project(v_bases, column_entries, "fabckj,fcvbj->fabkv")
     real_component, imag_part = apply_ranks(real_component, imag_part, ranks, rank_cap)
     row_terms = expand_terms(u_bases, real_component, imag_part, "fabcki,fabckv->fvai")
     row_terms = row_terms.reshape(local_freq, 2, virtual_source, tiles_row * tile_len)
-    row_grand_total = lax.psum(row_terms.astype(jnp.bfloat16), "tcol").astype(jnp.float32)
+    piece = tiles_row * tile_len // col_shards
+    row_terms = row_terms.reshape(2 * virtual_source, col_shards, piece).transpose(1, 0, 2)
+    row_terms = lax.all_to_all(
+        row_terms.astype(jnp.bfloat16), "tcol", split_axis=0, concat_axis=0, tiled=True
+    )
+    row_piece = jnp.sum(row_terms.astype(jnp.float32), axis=0).astype(jnp.bfloat16)
+    row_grand_total = lax.all_to_all(
+        jnp.broadcast_to(row_piece[None], (col_shards,) + row_piece.shape),
+        "tcol",
+        split_axis=0,
+        concat_axis=0,
+        tiled=True,
+    )
+    row_grand_total = row_grand_total.transpose(1, 0, 2).reshape(observed.shape)
+    row_grand_total = row_grand_total.astype(jnp.float32)
     residual = observed - row_grand_total
     row_data = residual.astype(jnp.bfloat16).reshape(
         local_freq, 2, virtual_source, tiles_row, tile_len
@@ -77,15 +102,21 @@
     real_component, imag_part = conj_project(u_bases, row_data, "fabcki,fcvai->fabkv")
     real_component, imag_part = apply_ranks(real_component, imag_part, ranks, rank_cap)
     back_terms = expand_terms(v_bases, real_component, imag_part, "fabckj,fabckv->fvbj")
-    back_terms = back_terms.reshape(local_freq, 2, virtual_source, tiles_col * tile_len)
-    col_total = lax.psum(back_terms.astype(jnp.bfloat16), "trow").astype(jnp.float32)
-    sub_len = back_terms.shape[3] // lax.axis_size("trow")
-    summed = lax.dynamic_slice_in_dim(col_total, lax.axis_index("trow") * sub_len, sub_len, 3)
-    packed = summed.astype(jnp.bfloat16)
+    back_terms = back_terms.reshape(2, freq_count, virtual_source // freq_count, tiles_col, tile_len)
+    back_terms = back_terms.transpose(1, 3, 0, 2, 4).astype(jnp.bfloat16)
+    back_terms = lax.all_to_all(
+        back_terms.reshape((freq_count * row_shards,) + back_terms.shape[2:]),
+        ("freq", "trow"),
+        split_axis=0,
+        concat_axis=0,
+        tiled=True,
+    )
+    back_terms = back_terms.reshape((freq_count, row_shards) + back_terms.shape[1:])
+    packed = jnp.sum(back_terms.astype(jnp.float32), axis=1).astype(jnp.bfloat16)
     values = jnp.einsum(
         "nuz,nuhr->hrz",
         basis_lookup_table,
-        lax.all_to_all(packed, "freq", split_axis=2, concat_axis=0, tiled=True),
+        packed,
         preferred_element_type=jnp.float32,
     )
     result = (values * (1.0 / math.sqrt(freq_count))).astype(jnp.bfloat16)

time: 230 us -> 76.8 us (0.33); the launches traced: 227 us -> 76.5 us
  waiting for transfers between devices: 168 us -> 17.2 us
  between operations: 14.3 us -> 0.9 us
  blocking collectives: 21.6 us -> 30 us
  starting transfers between devices: 10.9 us -> 17.1 us
  other arithmetic: 4.28 us -> 1.57 us
    psum x2 -> x0, waiting for transfers between devices: 161 us -> none  [the longest x1 111 us: shards(): lax.psum(row_terms.astype(jnp.bfloat16), 'tcol').astype(jnp.float32)]
    all_to_all x1 -> x2, blocking collectives: 13.5 us -> 30 us  [the longest x1 18.2 us: shards(): lax.all_to_all(row_terms.astype(jnp.bfloat16), 'tcol', split_axis=0, conc...]
    all_to_all x1 -> x2, waiting for transfers between devices: 6.5 us -> 17.2 us  [the longest x1 8.74 us: shards(): lax.all_to_all(spectrum.reshape((freq_count * row_shards,) + spectrum.sha...]
    all_gather x1 -> x0, blocking collectives: 8.05 us -> none  [shards(): spectrum = lax.all_gather(spectrum, 'trow', axis=3, tiled=True)]
    all_to_all x1 -> x2, starting transfers between devices: 10.9 us -> 17.1 us  [the longest x1 13.7 us: shards(): lax.all_to_all(spectrum.reshape((freq_count * row_shards,) + spectrum.sha...]
  transfers between devices with their start and end apart: 3 -> 2, of which waited for: 3 -> 2; matrix products, arithmetic and copies ran while one was open for 0% -> 0% of each run, Pallas kernels for 0% -> 0%
where the time goes in v1:
time: 76.8 us; the launch traced here: 76.5 us
  blocking collectives  30 us (39%)
  waiting for transfers between devices  17.2 us (22%)
  starting transfers between devices  17.1 us (22%)
  matrix products  7.7 us (10%)
  local copies, waits for them, and re-layouts  2 us (3%)
  other arithmetic  1.57 us (2%)
  between operations  0.9 us (1%)
    all_to_all x1, blocking collectives, shards(): lax.all_to_all(row_terms.astype(jnp.bfloat16), 'tcol', split_axis=0, conc...  18.2 us
    all_to_all x1, starting transfers between devices, shards(): lax.all_to_all(spectrum.reshape((freq_count * row_shards,) + spectrum.sha...  13.7 us
    all_to_all x1, blocking collectives, shards(): lax.all_to_all(back_terms.reshape((freq_count * row_shards,) + back_terms...  11.8 us
    all_to_all x1, waiting for transfers between devices, shards(): lax.all_to_all(spectrum.reshape((freq_count * row_shards,) + spectrum.sha...  8.74 us
    all_to_all x1, waiting for transfers between devices, shards(): lax.all_to_all(jnp.broadcast_to(row_piece[None], (col_shards,) + row_piec...  8.46 us
    all_to_all x1, starting transfers between devices, shards(): lax.all_to_all(jnp.broadcast_to(row_piece[None], (col_shards,) + row_piec...  3.41 us
    dot_general x1, matrix products, shards(): jnp.einsum('gzq,odq->gzod', basis_lookup_table, resident_traces, preferre...  1.77 us
    dot_general x2, matrix products, conj_project(): jnp.einsum(einsum_form, basis_set, swapped, preferred_element_type=jnp.fl...  1.6 us
  transfers between devices with their start and end apart: 2, of which 2 were waited for; matrix products, arithmetic and copies ran while one was open for 0% of the time, Pallas kernels for 0%

profile of v1, /device:TPU:1, one launch (start us, length us, event | category | flops | bytes accessed | tf_op | source)
XLA Modules:
  0.0 76.5 jit_solution(18179161584161999183)
XLA Ops:
  0.6 0.0 copy-start
  0.6 0.0 copy-start.2
  0.7 0.0 copy-start.3
  0.7 0.2 cosine_convert_fusion
  0.9 1.8 %fusion.20 = bf16[8,2,2,256]{3,0,2,1:T(8,128)(2,1)S(1)} fusion(bf16[2,1,256,1024]{3,2,1,0:T(8,128)(2,1)} %param.5, bf16[8,1,1024]{2,0,1:T(8,128)(2,1)S(1)} %get-tuple-element.21, bf16[8,1,1024]{2,0,1:T(8,128)(2,1)S(1)} %get-tuple-element.20), kind=kOutput, calls=%fused_computation.30 | convolution fusion | flops 16859136 | bytes 1097728 | tf_op jit(solution)/shard_map/gzq,odq->gzod/dot_general | solution.py:60
  2.7 0.7 broadcast_in_dim.4
  3.4 13.7 %all-to-all-start = ((bf16[32,2,2,256]{3,2,1,0:T(2,128)(2,1)}), bf16[32,2,2,256]{3,2,1,0:T(2,128)(2,1)S(1)}, u32[]{:S(2)}, u32[]{:S(2)}) async-start(bf16[32,2,2,256]{3,2,1,0:T(2,128)(2,1)} %bitcast.4), calls=%async_computation | async-start | bytes 131072 | tf_op jit(solution)/shard_map/all_to_all | solution.py:68
  17.1 0.0 copy-done.2
  17.1 0.1 fusion.48
  17.2 8.7 %all-to-all-done = bf16[32,2,2,256]{3,2,1,0:T(2,128)(2,1)S(1)} async-done(((bf16[32,2,2,256]{3,2,1,0:T(2,128)(2,1)}), bf16[32,2,2,256]{3,2,1,0:T(2,128)(2,1)S(1)}, u32[]{:S(2)}, u32[]{:S(2)}) %all-to-all-start) | async-done | bytes 65568 | tf_op jit(solution)/shard_map/all_to_all | solution.py:68
  26.1 0.0 copy-done.3
  26.1 0.8 %fusion.11 = bf16[1,8,4,1,32,16]{4,5,1,2,3,0:T(8,128)(2,1)S(1)} fusion(f32[8,4,32]{2,0,1:T(8,128)S(1)} %fusion.48, bf16[2,16,4,256,1]{3,1,0,2,4:T(8,128)(2,1)S(1)} %reshape.250, bf16[1,8,4,2,32,256]{5,4,3,2,1,0:T(8,128)(2,1)S(1)} %copy-done.3), kind=kOutput, calls=%fused_computation.18 | convolution fusion | flops 16809984 | bytes 1150976 | tf_op jit(solution)/shard_map/fabckj,fcvbj->fabkv/dot_general | solution.py:21
  26.8 0.8 %fusion.6 = bf16[1,8,4,32,16]{3,4,1,2,0:T(8,128)(2,1)S(1)} fusion(f32[8,4,32]{2,0,1:T(8,128)S(1)} %fusion.48, bf16[1,1,16,4,256]{4,2,1,3,0:T(8,128)(2,1)S(1)} %get-tuple-element.19, bf16[1,1,16,4,256]{4,2,1,3,0:T(8,128)(2,1)S(1)} %get-tuple-element.18, bf16[1,8,4,2,32,256]{5,4,3,2,1,0:T(8,128)(2,1)S(1)} %copy-done.3), kind=kOutput, calls=%fused_computation.11 | convolution fusion | flops 16941056 | bytes 1150976 | tf_op jit(solution)/shard_map/fabckj,fcvbj->fabkv/dot_general | solution.py:22
  27.7 0.1 maximum_bitcast_fusion
  27.8 0.0 copy-done
  27.8 0.3 fusion.15
  28.1 0.3 fusion.14
  28.7 18.2 %all_to_all.20 = bf16[16,32,128]{2,1,0:T(8,128)(2,1)S(1)} all-to-all(bf16[16,32,128]{2,1,0:T(8,128)(2,1)S(1)} %copy.71), channel_id=1, replica_groups=mesh['freq'=8,'trow'=4,'tcol'=16] {'tcol'}, dimensions={0} | all-to-all | bytes 262144 | tf_op jit(solution)/shard_map/all_to_all | solution.py:85
  46.8 0.0 copy-start.1
  46.9 0.7 broadcast_in_dim.5
  47.6 3.4 %all-to-all-start.2 = ((bf16[16,32,128]{2,1,0:T(8,128)(2,1)}), bf16[16,32,128]{2,1,0:T(8,128)(2,1)S(1)}, u32[]{:S(2)}, u32[]{:S(2)}) async-start(bf16[16,32,128]{2,1,0:T(8,128)(2,1)} %broadcast_in_dim.5), calls=%async_computation.2 | async-start | bytes 262144 | tf_op jit(solution)/shard_map/all_to_all | solution.py:89
  51.0 8.5 %all-to-all-done.2 = bf16[16,32,128]{2,1,0:T(8,128)(2,1)S(1)} async-done(((bf16[16,32,128]{2,1,0:T(8,128)(2,1)}), bf16[16,32,128]{2,1,0:T(8,128)(2,1)S(1)}, u32[]{:S(2)}, u32[]{:S(2)}) %all-to-all-start.2) | async-done | bytes 131104 | tf_op jit(solution)/shard_map/all_to_all | solution.py:89
  59.5 0.2 copy.72
  59.7 0.0 copy-done.1
  59.7 0.7 fusion.55
  60.5 0.8 %fusion.10 = bf16[1,8,4,1,32,16]{4,5,2,1,3,0:T(8,128)(2,1)S(1)} fusion(bf16[2,16,8,256,1]{3,2,1,0,4:T(8,128)(2,1)S(1)} %bitcast_bitcast_fusion, f32[8,4,32]{2,1,0:T(4,128)S(1)} %copy.74, bf16[1,8,4,2,32,256]{5,4,3,2,1,0:T(8,128)(2,1)S(1)} %copy-done), kind=kOutput, calls=%fused_computation.17 | convolution fusion | flops 16809984 | bytes 1216512 | tf_op jit(solution)/shard_map/fabcki,fcvai->fabkv/dot_general | solution.py:21
  61.3 0.8 %fusion.9 = bf16[8,16,4,32]{3,1,2,0:T(8,128)(2,1)S(1)} fusion(bf16[1,1,16,8,256]{4,2,1,3,0:T(8,128)(2,1)S(1)} %copy_negate_fusion, bf16[1,1,16,8,256]{4,2,1,3,0:T(8,128)(2,1)S(1)} %copy.102, f32[8,4,32]{2,1,0:T(4,128)S(1)} %copy.74, bf16[1,8,4,2,32,256]{5,4,3,2,1,0:T(8,128)(2,1)S(1)} %copy-done), kind=kOutput, calls=%fused_computation.14 | convolution fusion | flops 17072128 | bytes 1216512 | tf_op jit(solution)/shard_map/fabcki,fcvai->fabkv/dot_general | solution.py:22
  62.2 0.1 maximum_bitcast_fusion.2
  62.3 0.3 fusion.19
  62.6 0.3 fusion.18
  63.0 0.1 pad_maximum_fusion.1
  63.2 11.8 %all_to_all.21 = bf16[32,2,2,256]{3,2,1,0:T(2,128)(2,1)S(1)} all-to-all(bf16[32,2,2,256]{3,2,1,0:T(2,128)(2,1)S(1)} %bitcast.224), channel_id=1, replica_groups=mesh['freq'=8,'trow'=4,'tcol'=16] {'freq','trow'}, dimensions={0} | all-to-all | bytes 131072 | tf_op jit(solution)/shard_map/all_to_all | solution.py:107
  75.0 0.1 bitcast_reduce_fusion
  75.1 1.5 %fusion.1 = bf16[2,1,256,1024]{3,2,1,0:T(8,128)(2,1)} fusion(bf16[8,1,1024]{2,0,1:T(8,128)(2,1)S(1)} %get-tuple-element.21, bf16[8,1,1024]{2,0,1:T(8,128)(2,1)S(1)} %get-tuple-element.20, bf16[8,2,2,256]{3,2,1,0:T(2,128)(2,1)S(1)} %bitcast_reduce_fusion), kind=kOutput, calls=%fused_computation.2 | convolution fusion | flops 17842176 | bytes 1097728 | tf_op jit(solution)/shard_map/nuz,nuhr->hrz/dot_general | solution.py:116
  (24 shorter events, 0.6 us)
Async XLA Ops:
  0.6 27.2 %copy-start = (bf16[1,8,4,2,32,256]{5,4,3,2,1,0:T(8,128)(2,1)S(1)}, bf16[1,8,4,2,32,256]{5,4,3,2,1,0:T(8,128)(2,1)}, u32[]{:S(2)}) copy-start(bf16[1,8,4,2,32,256]{5,4,3,2,1,0:T(8,128)(2,1)} %param.6) | copy-start | bytes 3145732
  0.6 16.4 %copy-start.2 = (s32[1,8,4]{1,2,0:T(4,128)S(1)}, s32[1,8,4]{1,2,0:T(4,128)}, u32[]{:S(2)}) copy-start(s32[1,8,4]{1,2,0:T(4,128)} %param.8) | copy-start | bytes 388
  0.7 25.4 %copy-start.3 = (bf16[1,8,4,2,32,256]{5,4,3,2,1,0:T(8,128)(2,1)S(1)}, bf16[1,8,4,2,32,256]{5,4,3,2,1,0:T(8,128)(2,1)}, u32[]{:S(2)}) copy-start(bf16[1,8,4,2,32,256]{5,4,3,2,1,0:T(8,128)(2,1)} %param.7) | copy-start | bytes 3145732
  3.4 22.5 %all-to-all-start = ((bf16[32,2,2,256]{3,2,1,0:T(2,128)(2,1)}), bf16[32,2,2,256]{3,2,1,0:T(2,128)(2,1)S(1)}, u32[]{:S(2)}, u32[]{:S(2)}) async-start(bf16[32,2,2,256]{3,2,1,0:T(2,128)(2,1)} %bitcast.4), calls=%async_computation | async-start | bytes 131072 | tf_op jit(solution)/shard_map/all_to_all | solution.py:68
  46.8 12.8 %copy-start.1 = (f32[1,2,16,2048]{3,2,1,0:T(8,128)S(1)}, f32[1,2,16,2048]{3,2,1,0:T(8,128)}, u32[]{:S(2)}) copy-start(f32[1,2,16,2048]{3,2,1,0:T(8,128)} %param.9) | copy-start | bytes 786436
  47.6 11.9 %all-to-all-start.2 = ((bf16[16,32,128]{2,1,0:T(8,128)(2,1)}), bf16[16,32,128]{2,1,0:T(8,128)(2,1)S(1)}, u32[]{:S(2)}, u32[]{:S(2)}) async-start(bf16[16,32,128]{2,1,0:T(8,128)(2,1)} %broadcast_in_dim.5), calls=%async_computation.2 | async-start | bytes 262144 | tf_op jit(solution)/shard_map/all_to_all | solution.py:89

commit v2 on v0

v2 whole, which is shorter than its diff:
```python
import math

import jax
import jax.numpy as jnp
from jax import lax
from jax.experimental import pallas as pl
from jax.experimental.pallas import tpu as pltpu
from jax.sharding import PartitionSpec as P

FIRST_BIN = 40
LANES = 128
SUBLANES = 8
VMEM_LIMIT = 16 * 1024 * 1024


def dft_rows(freq_count, first_bin, trace_len):
    freq_bins = first_bin + jnp.arange(freq_count, dtype=jnp.int32)
    time_steps = jnp.arange(trace_len, dtype=jnp.int32)
    phase_index = freq_bins[:, None] * time_steps[None, :] % trace_len
    angles = phase_index.astype(jnp.float32) * (2.0 * math.pi / trace_len)
    return jnp.concatenate([jnp.cos(angles), -jnp.sin(angles)], axis=0).astype(jnp.bfloat16)


def contract_last(left, right):
    return lax.dot_general(
        left, right, (((1,), (1,)), ((), ())), preferred_element_type=jnp.float32
    )


def vmem_spec():
    return pl.BlockSpec(memory_space=pltpu.VMEM)


def any_spec():
    return pl.BlockSpec(memory_space=pl.ANY)


def params():
    return pltpu.CompilerParams(vmem_limit_bytes=VMEM_LIMIT)


def cost(flops, moved):
    return pl.CostEstimate(flops=flops, bytes_accessed=moved, transcendentals=0)


def spectrum_kernel(scale, copies_out, traces_ref, basis_ref, out_ref, held, rows, sems):
    sources, _, positions, _ = traces_ref.shape
    halves = positions // LANES
    freq_count = basis_ref.shape[0] // 2
    copies = []
    for g in range(sources):
        for h in range(halves):
            copy = pltpu.make_async_copy(
                traces_ref.at[g, 0, pl.ds(h * LANES, LANES)],
                held.at[g * halves + h],
                sems.at[g * halves + h],
            )
            copy.start()
            copies.append(copy)
    group = halves * 2 * sources
    for g in range(sources):
        for h in range(halves):
            copies[g * halves + h].wait()
            part = contract_last(basis_ref[...], held[g * halves + h]) * scale
            for c in range(2):
                rows[pl.ds((h * 2 + c) * sources + g, freq_count, stride=group), :] = part[
                    c * freq_count : (c + 1) * freq_count
                ]
    for f in range(freq_count):
        piece = rows[f * group : (f + 1) * group, :].astype(jnp.bfloat16)
        for r in range(copies_out):
            out_ref[f * copies_out + r] = piece


def combined(top, bottom, mask):
    lane = lax.broadcasted_iota(jnp.int32, top.shape, 1)
    first = (lane // 32) % 2 == 0

    def swapped(x):
        return jnp.where(
            first, -pltpu.roll(x, LANES - 32, 1), pltpu.roll(x, 32, 1)
        )

    new_top = (top - swapped(bottom)) * mask
    new_bottom = (bottom + swapped(top)) * mask
    return new_top.astype(jnp.bfloat16), new_bottom.astype(jnp.bfloat16)


def forward_kernel(spec_ref, v_ref, u_ref, mask_ref, out_ref, rows, held):
    chunks, group, _ = spec_ref.shape
    tiles_row, tiles_col = v_ref.shape[1:3]
    owners = chunks // tiles_col
    sources = group // 4
    virtual = owners * sources
    for n in range(chunks):
        rows[n * group : (n + 1) * group, :] = spec_ref[n].astype(jnp.float32)
    for b in range(tiles_col):
        for h in range(2):
            pieces = [
                rows[pl.ds(b * group + h * 2 * sources + i, owners, stride=tiles_col * group), :]
                for i in range(2 * sources)
            ]
            held[b * 2 * virtual : (b + 1) * 2 * virtual, h * LANES : (h + 1) * LANES] = (
                jnp.concatenate(pieces, axis=0).astype(jnp.bfloat16)
            )
    width = tiles_col * 64
    spectra = held[...]
    per_half = LANES // 64
    for a in range(tiles_row):
        bases = v_ref[0, a].reshape(width, v_ref.shape[5])
        products = contract_last(spectra, bases)
        tops, bottoms = [], []
        for h in range(width // LANES):
            lanes = slice(h * LANES, (h + 1) * LANES)
            lane = lax.broadcasted_iota(jnp.int32, (2 * virtual, LANES), 1)
            low = products[(2 * h) * 2 * virtual : (2 * h + 1) * 2 * virtual, lanes]
            high = products[(2 * h + 1) * 2 * virtual : (2 * h + 2) * 2 * virtual, lanes]
            chosen = jnp.where(lane < 64, low, high)
            top, bottom = combined(chosen[:virtual], chosen[virtual:], mask_ref[a : a + 1, lanes])
            tops.append(top)
            bottoms.append(bottom)
        left = jnp.concatenate(
            [jnp.concatenate(tops, axis=1), jnp.concatenate(bottoms, axis=1)], axis=0
        )
        terms = jnp.dot(
            left, u_ref[0, a].reshape(width, u_ref.shape[5]), preferred_element_type=jnp.float32
        ).astype(jnp.bfloat16)
        for h in range(2):
            out_ref[2 * a + h] = terms[:, h * LANES : (h + 1) * LANES]


def sum_kernel(sources, parts_ref, out_ref, rows):
    count, height, _ = parts_ref.shape
    total = parts_ref[0].astype(jnp.float32)
    for n in range(1, count):
        total = total + parts_ref[n].astype(jnp.float32)
    virtual = height // 2
    owners = virtual // sources
    for c in range(2):
        for g in range(sources):
            start = c * virtual + g * owners
            rows[pl.ds(c * virtual + g, owners, stride=sources), :] = total[start : start + owners]
    piece = rows[...].astype(jnp.bfloat16)
    for n in range(count):
        out_ref[n] = piece


def adjoint_kernel(
    sources, observed_ref, total_ref, u_ref, v_ref, mask_ref, residual_ref, out_ref, rows, ordered
):
    chunks, group, _ = out_ref.shape
    tiles_row, tiles_col = u_ref.shape[1:3]
    virtual = observed_ref.shape[2]
    owners = chunks // tiles_col
    width = tiles_col * 64
    total = None
    lane = lax.broadcasted_iota(jnp.int32, (2 * virtual, LANES), 1)
    nothing = jnp.zeros((2 * virtual, LANES), jnp.bfloat16)
    for a in range(tiles_row):
        data = []
        for h in range(2):
            n = 2 * a + h
            lanes = slice(n * LANES, (n + 1) * LANES)
            predicted = total_ref[n].astype(jnp.float32)
            parts = []
            for c in range(2):
                left = observed_ref[0, c, :, lanes] - predicted[c * virtual : (c + 1) * virtual]
                residual_ref[0, c, :, lanes] = left
                parts.append(left.astype(jnp.bfloat16))
            data.append(jnp.concatenate(parts, axis=0))
        products = contract_last(
            jnp.concatenate(data, axis=1), u_ref[0, a].reshape(width, u_ref.shape[5])
        )
        blocks = []
        for h in range(width // LANES):
            lanes = slice(h * LANES, (h + 1) * LANES)
            top, bottom = combined(
                products[:virtual, lanes], products[virtual:, lanes], mask_ref[a : a + 1, lanes]
            )
            both = jnp.concatenate([top, bottom], axis=0)
            for low in (True, False):
                chosen = jnp.where((lane < 64) == low, both, nothing)
                blocks.append(
                    jnp.concatenate([chosen if h == k else nothing for k in range(width // LANES)], axis=1)
                )
        terms = jnp.dot(
            jnp.concatenate(blocks, axis=0),
            v_ref[0, a].reshape(width, v_ref.shape[5]),
            preferred_element_type=jnp.float32,
        )
        total = terms if total is None else total + terms
    for h in range(2):
        rows[h] = total[:, h * LANES : (h + 1) * LANES]
    for b in range(tiles_col):
        for h in range(2):
            for c in range(2):
                for g in range(sources):
                    ordered[
                        pl.ds(
                            b * group + (h * 2 + c) * sources + g, owners, stride=tiles_col * group
                        ),
                        :,
                    ] = rows[h, pl.ds((b * 2 + c) * virtual + g, owners, stride=sources), :]
    for n in range(chunks):
        out_ref[n] = ordered[n * group : (n + 1) * group, :].astype(jnp.bfloat16)


def back_kernel(scale, copies_in, parts_ref, basis_ref, out_ref, rows):
    chunks, group, _ = parts_ref.shape
    freq_count = chunks // copies_in
    sources = group // 4
    for f in range(freq_count):
        total = parts_ref[f * copies_in].astype(jnp.float32)
        for r in range(1, copies_in):
            total = total + parts_ref[f * copies_in + r].astype(jnp.float32)
        rows[f * group : (f + 1) * group, :] = total
    basis = basis_ref[...]
    for g in range(sources):
        for h in range(2):
            spectra = jnp.concatenate(
                [
                    rows[pl.ds((h * 2 + c) * sources + g, freq_count, stride=group), :]
                    for c in range(2)
                ],
                axis=0,
            ).astype(jnp.bfloat16)
            values = lax.dot_general(
                spectra, basis, (((0,), (0,)), ((), ())), preferred_element_type=jnp.float32
            )
            out_ref[g, 0, h * LANES : (h + 1) * LANES, :] = (values * scale).astype(jnp.bfloat16)


def spectrum_chunks(traces, basis, row_shards):
    sources, _, positions, trace_len = traces.shape
    freq_count = basis.shape[0] // 2
    halves = positions // LANES
    group = halves * 2 * sources
    return pl.pallas_call(
        lambda *refs: spectrum_kernel(1.0 / math.sqrt(trace_len), row_shards, *refs),
        out_shape=jax.ShapeDtypeStruct((freq_count * row_shards, group, LANES), jnp.bfloat16),
        in_specs=[any_spec(), vmem_spec()],
        out_specs=vmem_spec(),
        scratch_shapes=[
            pltpu.VMEM((sources * halves, LANES, trace_len), jnp.bfloat16),
            pltpu.VMEM((freq_count * group, LANES), jnp.float32),
            pltpu.SemaphoreType.DMA((sources * halves,)),
        ],
        compiler_params=params(),
        cost_estimate=cost(2 * 2 * freq_count * traces.size, 2 * traces.size),
        name="spectrum",
    )(traces, basis)


def forward_chunks(spectra, v_bases, u_bases, mask, virtual):
    tiles_row, tiles_col = u_bases.shape[1:3]
    tile_len = u_bases.shape[5]
    return pl.pallas_call(
        forward_kernel,
        out_shape=jax.ShapeDtypeStruct((2 * tiles_row, 2 * virtual, LANES), jnp.bfloat16),
        in_specs=[vmem_spec()] * 4,
        out_specs=vmem_spec(),
        scratch_shapes=[
            pltpu.VMEM((spectra.shape[0] * spectra.shape[1], LANES), jnp.float32),
            pltpu.VMEM((tiles_col * 2 * virtual, tile_len), jnp.bfloat16),
        ],
        compiler_params=params(),
        cost_estimate=cost(8 * virtual * u_bases.size, 4 * u_bases.size),
        name="forward",
    )(spectra, v_bases, u_bases, mask)


def summed_chunks(parts, sources):
    return pl.pallas_call(
        lambda *refs: sum_kernel(sources, *refs),
        out_shape=jax.ShapeDtypeStruct(parts.shape, jnp.bfloat16),
        in_specs=[vmem_spec()],
        out_specs=vmem_spec(),
        scratch_shapes=[pltpu.VMEM(parts.shape[1:], jnp.float32)],
        compiler_params=params(),
        cost_estimate=cost(parts.size, 4 * parts.size),
        name="total",
    )(parts)


def adjoint_chunks(observed, total, u_bases, v_bases, mask, sources):
    tiles_col = u_bases.shape[2]
    tile_len = u_bases.shape[5]
    virtual = observed.shape[2]
    group = 4 * sources
    chunks = tiles_col * virtual // sources
    return pl.pallas_call(
        lambda *refs: adjoint_kernel(sources, *refs),
        out_shape=(
            jax.ShapeDtypeStruct(observed.shape, jnp.float32),
            jax.ShapeDtypeStruct((chunks, group, LANES), jnp.bfloat16),
        ),
        in_specs=[vmem_spec()] * 5,
        out_specs=(vmem_spec(), vmem_spec()),
        scratch_shapes=[
            pltpu.VMEM((tile_len // LANES, tiles_col * 2 * virtual, LANES), jnp.float32),
            pltpu.VMEM((chunks * group, LANES), jnp.float32),
        ],
        compiler_params=params(),
        cost_estimate=cost(8 * virtual * u_bases.size, 4 * u_bases.size),
        name="adjoint",
    )(observed, total, u_bases, v_bases, mask)


def back_traces(parts, basis, row_shards, shape):
    freq_count = basis.shape[0] // 2
    group = parts.shape[1]
    return pl.pallas_call(
        lambda *refs: back_kernel(1.0 / math.sqrt(freq_count), row_shards, *refs),
        out_shape=jax.ShapeDtypeStruct(shape, jnp.bfloat16),
        in_specs=[vmem_spec(), vmem_spec()],
        out_specs=vmem_spec(),
        scratch_shapes=[pltpu.VMEM((freq_count * group, LANES), jnp.float32)],
        compiler_params=params(),
        cost_estimate=cost(4 * freq_count * math.prod(shape), 2 * math.prod(shape)),
        name="back",
    )(parts, basis)


def shards(traces, u_bases, v_bases, ranks, observed):
    tiles_row, tiles_col = u_bases.shape[1:3]
    rank_cap = u_bases.shape[4]
    virtual = observed.shape[2]
    sources = traces.shape[0]
    freq_count = u_bases.shape[0] * lax.axis_size("freq")
    row_shards = lax.axis_size("trow")
    basis = dft_rows(freq_count, FIRST_BIN, traces.shape[3])
    mask = jnp.arange(rank_cap, dtype=jnp.int32) < ranks[0, :, :, None, None]
    mask = jnp.broadcast_to(mask, (tiles_row, tiles_col, 2, rank_cap))
    mask = mask.astype(jnp.float32).reshape(tiles_row, tiles_col * 2 * rank_cap)

    def exchange(chunks, axes):
        return lax.all_to_all(chunks, axes, split_axis=0, concat_axis=0, tiled=True)

    spectra = exchange(spectrum_chunks(traces, basis, row_shards), ("freq", "trow"))
    terms = exchange(forward_chunks(spectra, v_bases, u_bases, mask, virtual), "tcol")
    total = exchange(summed_chunks(terms, sources), "tcol")
    residual, back = adjoint_chunks(observed, total, u_bases, v_bases, mask, sources)
    back = exchange(back, ("freq", "trow"))
    return residual, back_traces(back, basis, row_shards, traces.shape)


def solution(mesh):
    placed = (
        P("freq", "tcol", "trow", None),
        P("freq", "trow", "tcol", None, None, None),
        P("freq", "trow", "tcol", None, None, None),
        P("freq", "trow", "tcol"),
        P("freq", None, None, "trow"),
    )
    return jax.shard_map(
        shards,
        mesh=mesh,
        in_specs=placed,
        out_specs=(P("freq", None, None, "trow"), P("freq", "tcol", "trow", None)),
        check_vma=False,
    )
```

time: 230 us -> 75.7 us (0.33)
  waiting for transfers between devices: 168 us -> 8.53 us
  blocking collectives: 21.6 us -> 42.2 us
  between operations: 14.3 us -> 0.71 us
  matrix products: 7.68 us -> 0 us
  Pallas kernels: 0 us -> 7.17 us
  other arithmetic: 4.28 us -> 0.3 us
  starting transfers between devices: 10.9 us -> 13.7 us
    psum x2 -> x0, waiting for transfers between devices: 161 us -> none  [the longest x1 111 us: shards(): lax.psum(row_terms.astype(jnp.bfloat16), 'tcol').astype(jnp.float32)]
    all_to_all x1 -> x3, blocking collectives: 13.5 us -> 42.2 us  [exchange(): return lax.all_to_all(chunks, axes, split_axis=0, concat_axis=0, tiled=True)]
    all_gather x1 -> x0, blocking collectives: 8.05 us -> none  [shards(): spectrum = lax.all_gather(spectrum, 'trow', axis=3, tiled=True)]
    dot_general x10 -> x0, matrix products: 7.68 us -> none  [the longest x1 1.77 us: shards(): jnp.einsum('gzq,odq->gzod', basis_lookup_table, resident_traces, preferre...]
    pallas_call x0 -> x5, Pallas kernels: none -> 7.17 us  [the longest x1 2.45 us: forward_chunks(): pl.pallas_call(forward_kernel, out_shape=jax.ShapeDtypeStruct((2 * tiles_...]
    all_to_all x1, starting transfers between devices: 10.9 us -> 13.7 us  [exchange(): return lax.all_to_all(chunks, axes, split_axis=0, concat_axis=0, tiled=True)]
    unnamed x11 -> x12, local copies, waits for them, and re-layouts: 0.07 us -> 2.52 us
    convert_element_type x3 -> x1, other arithmetic: 2.43 us -> 0.08 us  [shards(): mask = mask.astype(jnp.float32).reshape(tiles_row, tiles_col * 2 * rank_cap)]
  transfers between devices with their start and end apart: 3 -> 1, of which waited for: 3 -> 1; matrix products, arithmetic and copies ran while one was open for 0% -> 0% of each run, Pallas kernels for 0% -> 0%
where the time goes in v2:
time: 75.7 us; the launch traced here: 75.4 us
  blocking collectives  42.2 us (56%)
  starting transfers between devices  13.7 us (18%)
  waiting for transfers between devices  8.53 us (11%)
  Pallas kernels  7.17 us (9%)
  local copies, waits for them, and re-layouts  2.72 us (4%)
    all_to_all x3, blocking collectives, exchange(): return lax.all_to_all(chunks, axes, split_axis=0, concat_axis=0, tiled=True)  42.2 us
    all_to_all x1, starting transfers between devices, exchange(): return lax.all_to_all(chunks, axes, split_axis=0, concat_axis=0, tiled=True)  13.7 us
    all_to_all x1, waiting for transfers between devices, exchange(): return lax.all_to_all(chunks, axes, split_axis=0, concat_axis=0, tiled=True)  8.53 us
    unnamed x12, local copies, waits for them, and re-layouts  2.52 us
    pallas_call x1, Pallas kernels, forward_chunks(): pl.pallas_call(forward_kernel, out_shape=jax.ShapeDtypeStruct((2 * tiles_...  2.45 us
    pallas_call x1, Pallas kernels, spectrum_chunks(): pl.pallas_call(lambda *refs: spectrum_kernel(1.0 / math.sqrt(trace_len),...  1.76 us
  transfers between devices with their start and end apart: 1, of which 1 were waited for; matrix products, arithmetic and copies ran while one was open for 0% of the time, Pallas kernels for 0%

profile of v2, /device:TPU:1, one launch (start us, length us, event | category | flops | bytes accessed | tf_op | source)
XLA Modules:
  0.0 75.4 jit_solution(12419487915932977160)
XLA Ops:
  0.6 0.0 copy-start
  0.6 0.2 cosine_convert_fusion
  0.9 0.0 copy-start.3
  0.9 1.3 %copy-done.3 = bf16[2,1,256,1024]{3,2,1,0:T(8,128)(2,1)S(1)} copy-done((bf16[2,1,256,1024]{3,2,1,0:T(8,128)(2,1)S(1)}, bf16[2,1,256,1024]{3,2,1,0:T(8,128)(2,1)}, u32[]{:S(2)}) %copy-start.3) | copy-done | bytes 1048600
  2.2 1.8 %spectrum.1 = bf16[32,8,128]{2,1,0:T(8,128)(2,1)} custom-call(bf16[2,1,256,1024]{3,2,1,0:T(8,128)(2,1)S(1)} %copy-done.3, bf16[16,1024]{1,0:T(8,128)(2,1)S(1)} %pad_maximum_fusion.refs_1_), custom_call_target="tpu_custom_call" | custom-call | flops 16777216 | bytes 1048576 | tf_op jit(solution)/shard_map/spectrum/pallas_call | solution.py:238
  3.9 0.0 copy-start.5
  4.0 13.7 %all-to-all-start = ((bf16[32,8,128]{2,1,0:T(8,128)(2,1)}), bf16[32,8,128]{2,1,0:T(8,128)(2,1)S(1)}, u32[]{:S(2)}, u32[]{:S(2)}) async-start(bf16[32,8,128]{2,1,0:T(8,128)(2,1)} %spectrum.1), calls=%async_computation | async-start | bytes 131072 | tf_op jit(solution)/shard_map/all_to_all | solution.py:337
  17.7 0.0 copy-done.5
  17.7 0.1 copy.7
  17.8 0.1 fusion.6
  17.9 0.1 reshape.19.mask_ref.refs_4_
  18.0 8.5 %all-to-all-done.spec_ref = bf16[32,8,128]{2,1,0:T(8,128)(2,1)S(1)} async-done(((bf16[32,8,128]{2,1,0:T(8,128)(2,1)}), bf16[32,8,128]{2,1,0:T(8,128)(2,1)S(1)}, u32[]{:S(2)}, u32[]{:S(2)}) %all-to-all-start) | async-done | bytes 65568 | tf_op jit(solution)/shard_map/all_to_all | solution.py:337
  26.5 0.0 copy-done
  26.5 0.0 copy-start.1
  26.5 1.2 %copy-done.1 = bf16[1,8,4,2,32,256]{5,4,3,2,1,0:T(8,128)(2,1)S(1)} copy-done((bf16[1,8,4,2,32,256]{5,4,3,2,1,0:T(8,128)(2,1)S(1)}, bf16[1,8,4,2,32,256]{5,4,3,2,1,0:T(8,128)(2,1)}, u32[]{:S(2)}) %copy-start.1) | copy-done | bytes 1048600
  27.7 0.0 copy-start.2
  27.7 2.4 %forward.1 = bf16[16,32,128]{2,1,0:T(8,128)(2,1)S(1)} custom-call(bf16[32,8,128]{2,1,0:T(8,128)(2,1)S(1)} %all-to-all-done.spec_ref, bf16[1,8,4,2,32,256]{5,4,3,2,1,0:T(8,128)(2,1)S(1)} %copy-done, bf16[1,8,4,2,32,256]{5,4,3,2,1,0:T(8,128)(2,1)S(1)} %copy-done.1, f32[8,256]{1,0:T(8,128)S(1)} %reshape.19.mask_ref.refs_4_), custom_call_target="tpu_custom_call" | custom-call | flops 67108864 | bytes 2097152 | tf_op jit(solution)/shard_map/forward/pallas_call | solution.py:257
  30.2 18.2 %all_to_all.20.refs_0_ = bf16[16,32,128]{2,1,0:T(8,128)(2,1)S(1)} all-to-all(bf16[16,32,128]{2,1,0:T(8,128)(2,1)S(1)} %forward.1), channel_id=1, replica_groups=mesh['freq'=8,'trow'=4,'tcol'=16] {'tcol'}, dimensions={0} | all-to-all | bytes 262144 | tf_op jit(solution)/shard_map/all_to_all | solution.py:337
  48.4 0.0 copy-start.4
  48.4 11.7 %all_to_all.21.refs_1_ = bf16[16,32,128]{2,1,0:T(8,128)(2,1)S(1)} all-to-all(bf16[16,32,128]{2,1,0:T(8,128)(2,1)S(1)} %total.1), channel_id=1, replica_groups=mesh['freq'=8,'trow'=4,'tcol'=16] {'tcol'}, dimensions={0} | all-to-all | bytes 262144 | tf_op jit(solution)/shard_map/all_to_all | solution.py:337
  60.1 0.0 copy-done.2
  60.1 0.0 copy-done.4
  60.1 1.5 %adjoint.1 = (f32[1,2,16,2048]{3,2,1,0:T(8,128)}, bf16[32,8,128]{2,1,0:T(8,128)(2,1)S(1)}) custom-call(f32[1,2,16,2048]{3,2,1,0:T(8,128)S(1)} %copy-done.4, bf16[16,32,128]{2,1,0:T(8,128)(2,1)S(1)} %all_to_all.21.refs_1_, bf16[1,8,4,2,32,256]{5,4,3,2,1,0:T(8,128)(2,1)S(1)} %copy-done.2, bf16[1,8,4,2,32,256]{5,4,3,2,1,0:T(8,128)(2,1)S(1)} %copy-done, ...), custom_call_target="tpu_custom_call" | custom-call | flops 67108864 | bytes 2097152 | tf_op jit(solution)/shard_map/adjoint/pallas_call | solution.py:291
  61.6 12.3 %all_to_all.22.refs_0_ = bf16[32,8,128]{2,1,0:T(8,128)(2,1)S(1)} all-to-all(bf16[32,8,128]{2,1,0:T(8,128)(2,1)S(1)} %get-tuple-element.5), channel_id=1, replica_groups=mesh['freq'=8,'trow'=4,'tcol'=16] {'freq','trow'}, dimensions={0} | all-to-all | bytes 131072 | tf_op jit(solution)/shard_map/all_to_all | solution.py:337
  73.9 1.4 %back.1 = bf16[2,1,256,1024]{3,2,1,0:T(8,128)(2,1)} custom-call(bf16[32,8,128]{2,1,0:T(8,128)(2,1)S(1)} %all_to_all.22.refs_0_, bf16[16,1024]{1,0:T(8,128)(2,1)S(1)} %pad_maximum_fusion.refs_1_), custom_call_target="tpu_custom_call" | custom-call | flops 16777216 | bytes 1048576 | tf_op jit(solution)/shard_map/back/pallas_call | solution.py:312
  (4 shorter events, 0.1 us)
Async XLA Ops:
  0.6 25.9 %copy-start = (bf16[1,8,4,2,32,256]{5,4,3,2,1,0:T(8,128)(2,1)S(1)}, bf16[1,8,4,2,32,256]{5,4,3,2,1,0:T(8,128)(2,1)}, u32[]{:S(2)}) copy-start(bf16[1,8,4,2,32,256]{5,4,3,2,1,0:T(8,128)(2,1)} %refs_3_.1) | copy-start | bytes 3145732
  0.9 1.3 %copy-start.3 = (bf16[2,1,256,1024]{3,2,1,0:T(8,128)(2,1)S(1)}, bf16[2,1,256,1024]{3,2,1,0:T(8,128)(2,1)}, u32[]{:S(2)}) copy-start(bf16[2,1,256,1024]{3,2,1,0:T(8,128)(2,1)} %refs_0_.2) | copy-start | bytes 3145732
  3.9 13.8 %copy-start.5 = (s32[1,8,4]{1,2,0:T(4,128)S(1)}, s32[1,8,4]{1,2,0:T(4,128)}, u32[]{:S(2)}) copy-start(s32[1,8,4]{1,2,0:T(4,128)} %param.8) | copy-start | bytes 388
  4.0 22.6 %all-to-all-start = ((bf16[32,8,128]{2,1,0:T(8,128)(2,1)}), bf16[32,8,128]{2,1,0:T(8,128)(2,1)S(1)}, u32[]{:S(2)}, u32[]{:S(2)}) async-start(bf16[32,8,128]{2,1,0:T(8,128)(2,1)} %spectrum.1), calls=%async_computation | async-start | bytes 131072 | tf_op jit(solution)/shard_map/all_to_all | solution.py:337
  26.5 1.2 %copy-start.1 = (bf16[1,8,4,2,32,256]{5,4,3,2,1,0:T(8,128)(2,1)S(1)}, bf16[1,8,4,2,32,256]{5,4,3,2,1,0:T(8,128)(2,1)}, u32[]{:S(2)}) copy-start(bf16[1,8,4,2,32,256]{5,4,3,2,1,0:T(8,128)(2,1)} %refs_2_.1) | copy-start | bytes 3145732
  27.7 32.4 %copy-start.2 = (bf16[1,8,4,2,32,256]{5,4,3,2,1,0:T(8,128)(2,1)S(1)}, bf16[1,8,4,2,32,256]{5,4,3,2,1,0:T(8,128)(2,1)}, u32[]{:S(2)}) copy-start(bf16[1,8,4,2,32,256]{5,4,3,2,1,0:T(8,128)(2,1)} %refs_2_.1) | copy-start | bytes 3145732
  48.4 11.8 %copy-start.4 = (f32[1,2,16,2048]{3,2,1,0:T(8,128)S(1)}, f32[1,2,16,2048]{3,2,1,0:T(8,128)}, u32[]{:S(2)}) copy-start(f32[1,2,16,2048]{3,2,1,0:T(8,128)} %refs_0_.3) | copy-start | bytes 786436

commit v3 on v2

v3 whole, which is shorter than its diff:
```python
import math

import jax
import jax.numpy as jnp
from jax import lax
from jax.experimental import pallas as pl
from jax.experimental.pallas import tpu as pltpu
from jax.sharding import PartitionSpec as P

FIRST_BIN = 40
LANES = 128
SUBLANES = 8
VMEM_LIMIT = 16 * 1024 * 1024
VMEM_MOST = 60 * 1024 * 1024
VMEM_FETCH = 16 * 1024 * 1024


def dft_angles(freq_bins, time_steps, trace_len):
    phase_index = freq_bins * time_steps % trace_len
    return phase_index.astype(jnp.float32) * (2.0 * math.pi / trace_len)


def contract_last(left, right):
    return lax.dot_general(
        left, right, (((1,), (1,)), ((), ())), preferred_element_type=jnp.float32
    )


def vmem_spec():
    return pl.BlockSpec(memory_space=pltpu.VMEM)


def hbm_spec():
    return pl.BlockSpec(memory_space=pltpu.HBM)


def params(limit=VMEM_LIMIT):
    return pltpu.CompilerParams(vmem_limit_bytes=limit)


def cost(flops, moved):
    return pl.CostEstimate(flops=flops, bytes_accessed=moved, transcendentals=0)


def spectrum_kernel(scale, copies_out, traces_ref, out_ref, basis_ref, held, rows, sems):
    sources, _, positions, trace_len = traces_ref.shape
    halves = positions // LANES
    freq_count = basis_ref.shape[0] // 2
    copies = []
    for g in range(sources):
        for h in range(halves):
            copy = pltpu.make_async_copy(
                traces_ref.at[g, 0, pl.ds(h * LANES, LANES)],
                held.at[g * halves + h],
                sems.at[g * halves + h],
            )
            copy.start()
            copies.append(copy)
    row = lax.broadcasted_iota(jnp.int32, basis_ref.shape, 0)
    time = lax.broadcasted_iota(jnp.int32, basis_ref.shape, 1)
    angles = dft_angles(FIRST_BIN + row % freq_count, time, trace_len)
    basis_ref[...] = jnp.where(row < freq_count, jnp.cos(angles), -jnp.sin(angles)).astype(
        jnp.bfloat16
    )
    group = halves * 2 * sources
    for g in range(sources):
        for h in range(halves):
            copies[g * halves + h].wait()
    basis = basis_ref[...]
    part = contract_last(basis, held[...].reshape(sources * halves * LANES, trace_len)) * scale
    for g in range(sources):
        for h in range(halves):
            for c in range(2):
                rows[pl.ds((h * 2 + c) * sources + g, freq_count, stride=group), :] = part[
                    c * freq_count : (c + 1) * freq_count, (g * halves + h) * LANES : (g * halves + h + 1) * LANES
                ]
    for f in range(freq_count):
        piece = rows[f * group : (f + 1) * group, :].astype(jnp.bfloat16)
        for r in range(copies_out):
            out_ref[f * copies_out + r] = piece


def fetch_kernel(
    u_hbm, v_hbm, ranks_hbm, after, u_ref, v_ref, by_row_ref, by_col_ref, ranks_ref, sems
):
    del after
    tiles_row, tiles_col, _, rank_cap, _ = u_ref.shape[1:]
    rank_copy = pltpu.make_async_copy(ranks_hbm, ranks_ref, sems.at[0])
    v_copy = pltpu.make_async_copy(v_hbm, v_ref, sems.at[1])
    u_copy = pltpu.make_async_copy(u_hbm, u_ref, sems.at[2])
    rank_copy.start()
    v_copy.start()
    u_copy.start()
    rank_copy.wait()
    lane = lax.broadcasted_iota(jnp.int32, (1, LANES), 1)
    rank = lane % rank_cap
    low = lane < 2 * rank_cap
    for a in range(tiles_row):
        for b in range(0, tiles_col, 2):
            cap = jnp.where(low, ranks_ref[b, a], ranks_ref[b + 1, a])
            lanes = slice(b * 2 * rank_cap, (b + 2) * 2 * rank_cap)
            by_row_ref[a : a + 1, lanes] = jnp.where(rank < cap, 1.0, 0.0)
    for b in range(tiles_col):
        for a in range(0, tiles_row, 2):
            cap = jnp.where(low, ranks_ref[b, a], ranks_ref[b, a + 1])
            lanes = slice(a * 2 * rank_cap, (a + 2) * 2 * rank_cap)
            by_col_ref[b : b + 1, lanes] = jnp.where(rank < cap, 1.0, 0.0)
    v_copy.wait()
    u_copy.wait()


def combined(top, bottom, mask):
    lane = lax.broadcasted_iota(jnp.int32, top.shape, 1)
    first = (lane // 32) % 2 == 0

    def swapped(x):
        return jnp.where(
            first, -pltpu.roll(x, LANES - 32, 1), pltpu.roll(x, 32, 1)
        )

    new_top = (top - swapped(bottom)) * mask
    new_bottom = (bottom + swapped(top)) * mask
    return jnp.concatenate([new_top, new_bottom], axis=0).astype(jnp.bfloat16)


def forward_kernel(spec_ref, v_ref, u_ref, mask_ref, out_ref, rows):
    chunks, group, _ = spec_ref.shape
    tiles_row, tiles_col, _, rank_cap, tile_len = v_ref.shape[1:]
    owners = chunks // tiles_col
    sources = group // 4
    virtual = owners * sources
    for n in range(chunks):
        rows[n * group : (n + 1) * group, :] = spec_ref[n].astype(jnp.float32)
    products = []
    for b in range(tiles_col):
        spectra = jnp.concatenate(
            [
                jnp.concatenate(
                    [
                        rows[
                            pl.ds(b * group + h * 2 * sources + i, owners, stride=tiles_col * group),
                            :,
                        ]
                        for i in range(2 * sources)
                    ],
                    axis=0,
                )
                for h in range(2)
            ],
            axis=1,
        ).astype(jnp.bfloat16)
        bases = v_ref[0, :, b].reshape(tiles_row * 2 * rank_cap, tile_len)
        products.append(contract_last(spectra, bases))
    lane = lax.broadcasted_iota(jnp.int32, (2 * virtual, LANES), 1)
    nothing = jnp.zeros((2 * virtual, LANES), jnp.bfloat16)
    for p in range(tiles_row // 2):
        lanes = slice(p * LANES, (p + 1) * LANES)
        evens, odds = [], []
        for b in range(tiles_col):
            both = combined(
                products[b][:virtual, lanes],
                products[b][virtual:, lanes],
                mask_ref[b : b + 1, lanes],
            )
            evens.append(jnp.where(lane < 64, both, nothing))
            odds.append(jnp.where(lane < 64, nothing, both))
        left = jnp.concatenate(
            [jnp.concatenate(evens, axis=1), jnp.concatenate(odds, axis=1)], axis=0
        )
        bases = jnp.concatenate(
            [
                u_ref[0, 2 * p + i, b].reshape(2 * rank_cap, tile_len)
                for b in range(tiles_col)
                for i in range(2)
            ],
            axis=0,
        )
        terms = jnp.dot(left, bases, preferred_element_type=jnp.float32).astype(jnp.bfloat16)
        for i in range(2):
            for h in range(2):
                out_ref[2 * (2 * p + i) + h] = terms[
                    i * 2 * virtual : (i + 1) * 2 * virtual, h * LANES : (h + 1) * LANES
                ]


def sum_kernel(sources, parts_ref, out_ref, rows):
    count, height, _ = parts_ref.shape
    total = parts_ref[0].astype(jnp.float32)
    for n in range(1, count):
        total = total + parts_ref[n].astype(jnp.float32)
    virtual = height // 2
    owners = virtual // sources
    for c in range(2):
        for g in range(sources):
            start = c * virtual + g * owners
            rows[pl.ds(c * virtual + g, owners, stride=sources), :] = total[start : start + owners]
    piece = rows[...].astype(jnp.bfloat16)
    for n in range(count):
        out_ref[n] = piece


def adjoint_kernel(
    sources,
    observed_ref,
    total_ref,
    u_ref,
    v_ref,
    mask_ref,
    residual_ref,
    out_ref,
    rows,
    ordered,
    sems,
):
    chunks, group, _ = out_ref.shape
    tiles_row, tiles_col, _, rank_cap, tile_len = u_ref.shape[1:]
    virtual = observed_ref.shape[2]
    owners = chunks // tiles_col
    width = tiles_col * 2 * rank_cap
    pairs = width // LANES
    lane = lax.broadcasted_iota(jnp.int32, (2 * virtual, LANES), 1)
    nothing = jnp.zeros((2 * virtual, LANES), jnp.bfloat16)
    firsts = [[] for _ in range(pairs)]
    seconds = [[] for _ in range(pairs)]
    copies = []
    for a in range(tiles_row):
        data = []
        for h in range(2):
            n = 2 * a + h
            lanes = slice(n * LANES, (n + 1) * LANES)
            predicted = total_ref[n].astype(jnp.float32)
            parts = []
            for c in range(2):
                left = observed_ref[0, c, :, lanes] - predicted[c * virtual : (c + 1) * virtual]
                residual_ref[0, c, :, lanes] = left
                parts.append(left.astype(jnp.bfloat16))
            data.append(jnp.concatenate(parts, axis=0))
        products = contract_last(
            jnp.concatenate(data, axis=1), u_ref[0, a].reshape(width, tile_len)
        )
        for h in range(pairs):
            lanes = slice(h * LANES, (h + 1) * LANES)
            both = combined(
                products[:virtual, lanes], products[virtual:, lanes], mask_ref[a : a + 1, lanes]
            )
            firsts[h].append(jnp.where(lane < 64, both, nothing))
            seconds[h].append(jnp.where(lane < 64, nothing, both))
    for h in range(pairs):
        left = jnp.concatenate(
            [jnp.concatenate(firsts[h], axis=1), jnp.concatenate(seconds[h], axis=1)], axis=0
        )
        bases = v_ref[0, :, 2 * h : 2 * h + 2].reshape(tiles_row * LANES, tile_len)
        terms = jnp.dot(left, bases, preferred_element_type=jnp.float32)
        for k in range(2):
            rows[k, h * 4 * virtual : (h + 1) * 4 * virtual, :] = terms[:, k * LANES : (k + 1) * LANES]
    for b in range(tiles_col):
        for h in range(2):
            for c in range(2):
                for g in range(sources):
                    ordered[
                        pl.ds(
                            b * group + (h * 2 + c) * sources + g, owners, stride=tiles_col * group
                        ),
                        :,
                    ] = rows[h, pl.ds((b * 2 + c) * virtual + g, owners, stride=sources), :]
    for n in range(chunks):
        out_ref[n] = ordered[n * group : (n + 1) * group, :].astype(jnp.bfloat16)
    for copy in copies:
        copy.wait()


def back_kernel(
    scale, copies_in, residual_ref, parts_ref, basis_ref, residual_hbm, out_hbm, rows, held, sems
):
    pieces = held.shape[0]
    kept = pltpu.make_async_copy(residual_ref, residual_hbm, sems.at[pieces])
    kept.start()
    chunks, group, _ = parts_ref.shape
    freq_count = chunks // copies_in
    sources = group // 4
    for f in range(freq_count):
        total = parts_ref[f * copies_in].astype(jnp.float32)
        for r in range(1, copies_in):
            total = total + parts_ref[f * copies_in + r].astype(jnp.float32)
        rows[f * group : (f + 1) * group, :] = total
    basis = basis_ref[...]
    copies = [kept]
    for g in range(sources):
        for h in range(2):
            spectra = jnp.concatenate(
                [
                    rows[pl.ds((h * 2 + c) * sources + g, freq_count, stride=group), :]
                    for c in range(2)
                ],
                axis=0,
            ).astype(jnp.bfloat16)
            values = lax.dot_general(
                spectra, basis, (((0,), (0,)), ((), ())), preferred_element_type=jnp.float32
            )
            held[g * 2 + h] = (values * scale).astype(jnp.bfloat16)
            copy = pltpu.make_async_copy(
                held.at[g * 2 + h],
                out_hbm.at[g, 0, pl.ds(h * LANES, LANES)],
                sems.at[g * 2 + h],
            )
            copy.start()
            copies.append(copy)
    for copy in copies:
        copy.wait()


def spectrum_chunks(traces, freq_count, row_shards):
    sources, _, positions, trace_len = traces.shape
    halves = positions // LANES
    group = halves * 2 * sources
    return pl.pallas_call(
        lambda *refs: spectrum_kernel(1.0 / math.sqrt(trace_len), row_shards, *refs),
        out_shape=(
            jax.ShapeDtypeStruct((freq_count * row_shards, group, LANES), jnp.bfloat16),
            jax.ShapeDtypeStruct((2 * freq_count, trace_len), jnp.bfloat16),
        ),
        in_specs=[hbm_spec()],
        out_specs=(vmem_spec(), vmem_spec()),
        scratch_shapes=[
            pltpu.VMEM((sources * halves, LANES, trace_len), jnp.bfloat16),
            pltpu.VMEM((freq_count * group, LANES), jnp.float32),
            pltpu.SemaphoreType.DMA((sources * halves,)),
        ],
        compiler_params=params(VMEM_MOST),
        cost_estimate=cost(2 * 2 * freq_count * traces.size, 2 * traces.size),
        name="spectrum",
    )(traces)


def fetched(u_bases, v_bases, ranks, after):
    tiles_row, tiles_col, _, rank_cap, _ = u_bases.shape[1:]
    return pl.pallas_call(
        fetch_kernel,
        out_shape=(
            jax.ShapeDtypeStruct(u_bases.shape, jnp.bfloat16),
            jax.ShapeDtypeStruct(v_bases.shape, jnp.bfloat16),
            jax.ShapeDtypeStruct((tiles_row, tiles_col * 2 * rank_cap), jnp.float32),
            jax.ShapeDtypeStruct((tiles_col, tiles_row * 2 * rank_cap), jnp.float32),
        ),
        in_specs=[hbm_spec()] * 4,
        out_specs=(vmem_spec(),) * 4,
        scratch_shapes=[
            pltpu.SMEM((tiles_col, tiles_row), jnp.int32),
            pltpu.SemaphoreType.DMA((3,)),
        ],
        compiler_params=params(VMEM_FETCH),
        cost_estimate=cost(0, 4 * u_bases.size),
        name="fetch",
    )(u_bases, v_bases, ranks, after)


def forward_chunks(spectra, v_bases, u_bases, mask, virtual):
    tiles_row = u_bases.shape[1]
    return pl.pallas_call(
        forward_kernel,
        out_shape=jax.ShapeDtypeStruct((2 * tiles_row, 2 * virtual, LANES), jnp.bfloat16),
        in_specs=[vmem_spec()] * 4,
        out_specs=vmem_spec(),
        scratch_shapes=[
            pltpu.VMEM((spectra.shape[0] * spectra.shape[1], LANES), jnp.float32),
        ],
        compiler_params=params(),
        cost_estimate=cost(8 * virtual * u_bases.size, 4 * u_bases.size),
        name="forward",
    )(spectra, v_bases, u_bases, mask)


def summed_chunks(parts, sources):
    return pl.pallas_call(
        lambda *refs: sum_kernel(sources, *refs),
        out_shape=jax.ShapeDtypeStruct(parts.shape, jnp.bfloat16),
        in_specs=[vmem_spec()],
        out_specs=vmem_spec(),
        scratch_shapes=[pltpu.VMEM(parts.shape[1:], jnp.float32)],
        compiler_params=params(),
        cost_estimate=cost(parts.size, 4 * parts.size),
        name="total",
    )(parts)


def adjoint_chunks(observed, total, u_bases, v_bases, mask, sources):
    tiles_col = u_bases.shape[2]
    tile_len = u_bases.shape[5]
    virtual = observed.shape[2]
    group = 4 * sources
    chunks = tiles_col * virtual // sources
    return pl.pallas_call(
        lambda *refs: adjoint_kernel(sources, *refs),
        out_shape=(
            jax.ShapeDtypeStruct(observed.shape, jnp.float32),
            jax.ShapeDtypeStruct((chunks, group, LANES), jnp.bfloat16),
        ),
        in_specs=[vmem_spec()] * 5,
        out_specs=(vmem_spec(), vmem_spec()),
        scratch_shapes=[
            pltpu.VMEM((tile_len // LANES, tiles_col * 2 * virtual, LANES), jnp.float32),
            pltpu.VMEM((chunks * group, LANES), jnp.float32),
            pltpu.SemaphoreType.DMA((u_bases.shape[1] // 4,)),
        ],
        compiler_params=params(),
        cost_estimate=cost(8 * virtual * u_bases.size, 4 * u_bases.size),
        name="adjoint",
    )(observed, total, u_bases, v_bases, mask)


def back_traces(residual, parts, basis, row_shards, shape):
    freq_count = basis.shape[0] // 2
    group = parts.shape[1]
    pieces = shape[0] * shape[2] // LANES
    return pl.pallas_call(
        lambda *refs: back_kernel(1.0 / math.sqrt(freq_count), row_shards, *refs),
        out_shape=(
            jax.ShapeDtypeStruct(residual.shape, jnp.float32),
            jax.ShapeDtypeStruct(shape, jnp.bfloat16),
        ),
        in_specs=[vmem_spec()] * 3,
        out_specs=(hbm_spec(), hbm_spec()),
        scratch_shapes=[
            pltpu.VMEM((freq_count * group, LANES), jnp.float32),
            pltpu.VMEM((pieces, LANES, shape[3]), jnp.bfloat16),
            pltpu.SemaphoreType.DMA((pieces + 1,)),
        ],
        compiler_params=params(),
        cost_estimate=cost(4 * freq_count * math.prod(shape), 2 * math.prod(shape)),
        name="back",
    )(residual, parts, basis)


def shards(traces, u_bases, v_bases, ranks, observed):
    virtual = observed.shape[2]
    sources = traces.shape[0]
    freq_count = u_bases.shape[0] * lax.axis_size("freq")
    row_shards = lax.axis_size("trow")

    def exchange(chunks, axes):
        return lax.all_to_all(chunks, axes, split_axis=0, concat_axis=0, tiled=True)

    spectra, basis = spectrum_chunks(traces, freq_count, row_shards)
    u_held, v_held, by_row, by_col = fetched(u_bases, v_bases, ranks[0].T, spectra)
    spectra = exchange(spectra, ("freq", "trow"))
    terms = exchange(forward_chunks(spectra, v_held, u_held, by_col, virtual), "tcol")
    total = exchange(summed_chunks(terms, sources), "tcol")
    residual, back = adjoint_chunks(observed, total, u_held, v_held, by_row, sources)
    back = exchange(back, ("freq", "trow"))
    return back_traces(residual, back, basis, row_shards, traces.shape)


def solution(mesh):
    placed = (
        P("freq", "tcol", "trow", None),
        P("freq", "trow", "tcol", None, None, None),
        P("freq", "trow", "tcol", None, None, None),
        P("freq", "trow", "tcol"),
        P("freq", None, None, "trow"),
    )
    return jax.shard_map(
        shards,
        mesh=mesh,
        in_specs=placed,
        out_specs=(P("freq", None, None, "trow"), P("freq", "tcol", "trow", None)),
        check_vma=False,
    )
```

time: 75.7 us -> 71.2 us (0.941)
  waiting for transfers between devices: 8.53 us -> 6.94 us
  local copies, waits for them, and re-layouts: 2.72 us -> 1.25 us
  Pallas kernels: 7.17 us -> 5.78 us
    pallas_call x1, Pallas kernels: 2.45 us -> 0.73 us  [forward_chunks(): pl.pallas_call(forward_kernel, out_shape=jax.ShapeDtypeStruct((2 * tiles_...]
    all_to_all x1, waiting for transfers between devices: 8.53 us -> 6.94 us  [exchange(): return lax.all_to_all(chunks, axes, split_axis=0, concat_axis=0, tiled=True)]
    unnamed x12, local copies, waits for them, and re-layouts: 2.52 us -> 1.25 us
  transfers between devices with their start and end apart: 1 -> 1, of which waited for: 1 -> 1; matrix products, arithmetic and copies ran while one was open for 0% -> 0% of each run, Pallas kernels for 0% -> 1%
where the time goes in v3:
time: 71.2 us; the launch traced here: 70.7 us
  blocking collectives  42.2 us (59%)
  starting transfers between devices  13.9 us (20%)
  waiting for transfers between devices  6.94 us (10%)
  Pallas kernels  5.78 us (8%)
  local copies, waits for them, and re-layouts  1.25 us (2%)
  between operations  0.73 us (1%)
    all_to_all x3, blocking collectives, exchange(): return lax.all_to_all(chunks, axes, split_axis=0, concat_axis=0, tiled=True)  42.2 us
    all_to_all x1, starting transfers between devices, exchange(): return lax.all_to_all(chunks, axes, split_axis=0, concat_axis=0, tiled=True)  13.9 us
    all_to_all x1, waiting for transfers between devices, exchange(): return lax.all_to_all(chunks, axes, split_axis=0, concat_axis=0, tiled=True)  6.94 us
    pallas_call x1, Pallas kernels, spectrum_chunks(): pl.pallas_call(lambda *refs: spectrum_kernel(1.0 / math.sqrt(trace_len),...  2.34 us
  transfers between devices with their start and end apart: 1, of which 1 were waited for; matrix products, arithmetic and copies ran while one was open for 0% of the time, Pallas kernels for 1%

profile of v3, /device:TPU:1, one launch (start us, length us, event | category | flops | bytes accessed | tf_op | source)
XLA Modules:
  0.0 70.7 jit_solution(7956993533196341287)
XLA Ops:
  0.6 0.0 copy-start
  0.6 2.3 %spectrum.1 = (bf16[32,8,128]{2,1,0:T(8,128)(2,1)}, bf16[16,1024]{1,0:T(8,128)(2,1)}) custom-call(bf16[2,1,256,1024]{3,2,1,0:T(8,128)(2,1)} %refs_0_.2), custom_call_target="tpu_custom_call" | custom-call | flops 16777216 | bytes 1048576 | tf_op jit(solution)/shard_map/spectrum/pallas_call | solution.py:316
  3.0 0.0 copy-start.3
  3.0 0.0 copy-start.5
  3.0 13.9 %all-to-all-start = ((bf16[32,8,128]{2,1,0:T(8,128)(2,1)}), bf16[32,8,128]{2,1,0:T(8,128)(2,1)S(1)}, u32[]{:S(2)}, u32[]{:S(2)}) async-start(bf16[32,8,128]{2,1,0:T(8,128)(2,1)} %get-tuple-element.10.after), calls=%async_computation | async-start | bytes 131072 | tf_op jit(solution)/shard_map/all_to_all | solution.py:441
  16.9 0.0 copy-done
  16.9 0.0 copy-done.3
  16.9 0.0 copy-done.5
  16.9 0.0 copy-start.1
  16.9 1.2 %copy-done.1 = bf16[1,8,4,2,32,256]{5,4,3,2,1,0:T(8,128)(2,1)S(1)} copy-done((bf16[1,8,4,2,32,256]{5,4,3,2,1,0:T(8,128)(2,1)S(1)}, bf16[1,8,4,2,32,256]{5,4,3,2,1,0:T(8,128)(2,1)}, u32[]{:S(2)}) %copy-start.1) | copy-done | bytes 1048600
  18.1 0.6 fetch.1
  18.8 6.9 %all-to-all-done.spec_ref = bf16[32,8,128]{2,1,0:T(8,128)(2,1)S(1)} async-done(((bf16[32,8,128]{2,1,0:T(8,128)(2,1)}), bf16[32,8,128]{2,1,0:T(8,128)(2,1)S(1)}, u32[]{:S(2)}, u32[]{:S(2)}) %all-to-all-start) | async-done | bytes 65568 | tf_op jit(solution)/shard_map/all_to_all | solution.py:441
  25.7 0.7 %forward.1 = bf16[16,32,128]{2,1,0:T(8,128)(2,1)S(1)} custom-call(bf16[32,8,128]{2,1,0:T(8,128)(2,1)S(1)} %all-to-all-done.spec_ref, bf16[1,8,4,2,32,256]{5,4,3,2,1,0:T(8,128)(2,1)S(1)} %get-tuple-element.11.v_ref.refs_3_, bf16[1,8,4,2,32,256]{5,4,3,2,1,0:T(8,128)(2,1)S(1)} %get-tuple-element.12.u_ref.refs_2_, f32[4,512]{1,0:T(4,128)S(1)} %get-tuple-element.13.mask_ref), custom_call_target="tpu_custom_call" | custom-call | flops 67108864 | bytes 2097152 | tf_op jit(solution)/shard_map/forward/pallas_call | solution.py:359
  26.4 18.2 %all_to_all.20.refs_0_ = bf16[16,32,128]{2,1,0:T(8,128)(2,1)S(1)} all-to-all(bf16[16,32,128]{2,1,0:T(8,128)(2,1)S(1)} %forward.1), channel_id=1, replica_groups=mesh['freq'=8,'trow'=4,'tcol'=16] {'tcol'}, dimensions={0} | all-to-all | bytes 262144 | tf_op jit(solution)/shard_map/all_to_all | solution.py:441
  44.6 0.0 copy-start.2
  44.7 11.7 %all_to_all.21.refs_1_ = bf16[16,32,128]{2,1,0:T(8,128)(2,1)S(1)} all-to-all(bf16[16,32,128]{2,1,0:T(8,128)(2,1)S(1)} %total.1), channel_id=1, replica_groups=mesh['freq'=8,'trow'=4,'tcol'=16] {'tcol'}, dimensions={0} | all-to-all | bytes 262144 | tf_op jit(solution)/shard_map/all_to_all | solution.py:441
  56.4 0.0 copy-done.2
  56.4 0.8 %adjoint.1 = (f32[1,2,16,2048]{3,2,1,0:T(8,128)S(1)}, bf16[32,8,128]{2,1,0:T(8,128)(2,1)S(1)}) custom-call(f32[1,2,16,2048]{3,2,1,0:T(8,128)S(1)} %copy-done.2, bf16[16,32,128]{2,1,0:T(8,128)(2,1)S(1)} %all_to_all.21.refs_1_, bf16[1,8,4,2,32,256]{5,4,3,2,1,0:T(8,128)(2,1)S(1)} %get-tuple-element.12.u_ref.refs_2_, ...), custom_call_target="tpu_custom_call" | custom-call | flops 67108864 | bytes 2097152 | tf_op jit(solution)/shard_map/adjoint/pallas_call | solution.py:392
  57.2 0.0 copy-start.4
  57.2 12.3 %all_to_all.22.refs_1_ = bf16[32,8,128]{2,1,0:T(8,128)(2,1)S(1)} all-to-all(bf16[32,8,128]{2,1,0:T(8,128)(2,1)S(1)} %get-tuple-element.16), channel_id=1, replica_groups=mesh['freq'=8,'trow'=4,'tcol'=16] {'freq','trow'}, dimensions={0} | all-to-all | bytes 131072 | tf_op jit(solution)/shard_map/all_to_all | solution.py:441
  69.5 0.0 copy-done.4
  69.5 1.3 %back.1 = (f32[1,2,16,2048]{3,2,1,0:T(8,128)}, bf16[2,1,256,1024]{3,2,1,0:T(8,128)(2,1)}) custom-call(f32[1,2,16,2048]{3,2,1,0:T(8,128)S(1)} %get-tuple-element.15.refs_0_, bf16[32,8,128]{2,1,0:T(8,128)(2,1)S(1)} %all_to_all.22.refs_1_, bf16[16,1024]{1,0:T(8,128)(2,1)S(1)} %copy-done.4), custom_call_target="tpu_custom_call" | custom-call | flops 16777216 | bytes 1048576 | tf_op jit(solution)/shard_map/back/pallas_call | solution.py:415
  (1 shorter events, 0.0 us)
Async XLA Ops:
  0.6 16.3 %copy-start = (bf16[1,8,4,2,32,256]{5,4,3,2,1,0:T(8,128)(2,1)S(1)}, bf16[1,8,4,2,32,256]{5,4,3,2,1,0:T(8,128)(2,1)}, u32[]{:S(2)}) copy-start(bf16[1,8,4,2,32,256]{5,4,3,2,1,0:T(8,128)(2,1)} %u_hbm.1) | copy-start | bytes 3145732
  3.0 13.9 %copy-start.3 = (bf16[32,8,128]{2,1,0:T(8,128)(2,1)S(1)}, bf16[32,8,128]{2,1,0:T(8,128)(2,1)}, u32[]{:S(2)}) copy-start(bf16[32,8,128]{2,1,0:T(8,128)(2,1)} %get-tuple-element.10.after) | copy-start | bytes 196612
  3.0 13.9 %copy-start.5 = (s32[1,8,4]{1,2,0:T(4,128)S(1)}, s32[1,8,4]{1,2,0:T(4,128)}, u32[]{:S(2)}) copy-start(s32[1,8,4]{1,2,0:T(4,128)} %param.8) | copy-start | bytes 388
  3.0 22.7 %all-to-all-start = ((bf16[32,8,128]{2,1,0:T(8,128)(2,1)}), bf16[32,8,128]{2,1,0:T(8,128)(2,1)S(1)}, u32[]{:S(2)}, u32[]{:S(2)}) async-start(bf16[32,8,128]{2,1,0:T(8,128)(2,1)} %get-tuple-element.10.after), calls=%async_computation | async-start | bytes 131072 | tf_op jit(solution)/shard_map/all_to_all | solution.py:441
  16.9 1.2 %copy-start.1 = (bf16[1,8,4,2,32,256]{5,4,3,2,1,0:T(8,128)(2,1)S(1)}, bf16[1,8,4,2,32,256]{5,4,3,2,1,0:T(8,128)(2,1)}, u32[]{:S(2)}) copy-start(bf16[1,8,4,2,32,256]{5,4,3,2,1,0:T(8,128)(2,1)} %v_hbm.1) | copy-start | bytes 3145732
  44.6 11.8 %copy-start.2 = (f32[1,2,16,2048]{3,2,1,0:T(8,128)S(1)}, f32[1,2,16,2048]{3,2,1,0:T(8,128)}, u32[]{:S(2)}) copy-start(f32[1,2,16,2048]{3,2,1,0:T(8,128)} %refs_0_.3) | copy-start | bytes 786436
  57.2 12.3 %copy-start.4 = (bf16[16,1024]{1,0:T(8,128)(2,1)S(1)}, bf16[16,1024]{1,0:T(8,128)(2,1)}, u32[]{:S(2)}) copy-start(bf16[16,1024]{1,0:T(8,128)(2,1)} %get-tuple-element.17.refs_2_) | copy-start | bytes 98308

commit v4 on v3

--- a/solution.py
+++ b/solution.py
@@ -11,8 +11,6 @@
 LANES = 128
 SUBLANES = 8
 VMEM_LIMIT = 16 * 1024 * 1024
-VMEM_MOST = 60 * 1024 * 1024
-VMEM_FETCH = 16 * 1024 * 1024
 
 
 def dft_angles(freq_bins, time_steps, trace_len):
@@ -34,63 +32,65 @@
     return pl.BlockSpec(memory_space=pltpu.HBM)
 
 
-def params(limit=VMEM_LIMIT):
-    return pltpu.CompilerParams(vmem_limit_bytes=limit)
+def in_hbm(array):
+    return pltpu.with_memory_space_constraint(array, pltpu.HBM)
+
+
+def params():
+    return pltpu.CompilerParams(vmem_limit_bytes=VMEM_LIMIT)
 
 
 def cost(flops, moved):
     return pl.CostEstimate(flops=flops, bytes_accessed=moved, transcendentals=0)
 
 
-def spectrum_kernel(scale, copies_out, traces_ref, out_ref, basis_ref, held, rows, sems):
-    sources, _, positions, trace_len = traces_ref.shape
+def spectrum_kernel(
+    scale,
+    copies_out,
+    traces_hbm,
+    u_hbm,
+    v_hbm,
+    ranks_hbm,
+    out_ref,
+    basis_ref,
+    u_ref,
+    v_ref,
+    by_row_ref,
+    by_col_ref,
+    held,
+    rows,
+    ranks_ref,
+    sems,
+):
+    sources, _, positions, trace_len = traces_hbm.shape
     halves = positions // LANES
     freq_count = basis_ref.shape[0] // 2
+    tiles_row, tiles_col, _, rank_cap, _ = u_ref.shape[1:]
+    rank_copy = pltpu.make_async_copy(ranks_hbm, ranks_ref, sems.at[0])
+    v_copy = pltpu.make_async_copy(v_hbm, v_ref, sems.at[1])
+    u_copy = pltpu.make_async_copy(u_hbm, u_ref, sems.at[2])
     copies = []
     for g in range(sources):
         for h in range(halves):
-            copy = pltpu.make_async_copy(
-                traces_ref.at[g, 0, pl.ds(h * LANES, LANES)],
-                held.at[g * halves + h],
-                sems.at[g * halves + h],
+            copies.append(
+                pltpu.make_async_copy(
+                    traces_hbm.at[g, 0, pl.ds(h * LANES, LANES)],
+                    held.at[g * halves + h],
+                    sems.at[3 + g * halves + h],
+                )
             )
-            copy.start()
-            copies.append(copy)
+    for copy in copies:
+        copy.start()
+    rank_copy.start()
+    v_copy.start()
+    u_copy.start()
+
     row = lax.broadcasted_iota(jnp.int32, basis_ref.shape, 0)
     time = lax.broadcasted_iota(jnp.int32, basis_ref.shape, 1)
     angles = dft_angles(FIRST_BIN + row % freq_count, time, trace_len)
     basis_ref[...] = jnp.where(row < freq_count, jnp.cos(angles), -jnp.sin(angles)).astype(
         jnp.bfloat16
     )
-    group = halves * 2 * sources
-    for g in range(sources):
-        for h in range(halves):
-            copies[g * halves + h].wait()
-    basis = basis_ref[...]
-    part = contract_last(basis, held[...].reshape(sources * halves * LANES, trace_len)) * scale
-    for g in range(sources):
-        for h in range(halves):
-            for c in range(2):
-                rows[pl.ds((h * 2 + c) * sources + g, freq_count, stride=group), :] = part[
-                    c * freq_count : (c + 1) * freq_count, (g * halves + h) * LANES : (g * halves + h + 1) * LANES
-                ]
-    for f in range(freq_count):
-        piece = rows[f * group : (f + 1) * group, :].astype(jnp.bfloat16)
-        for r in range(copies_out):
-            out_ref[f * copies_out + r] = piece
-
-
-def fetch_kernel(
-    u_hbm, v_hbm, ranks_hbm, after, u_ref, v_ref, by_row_ref, by_col_ref, ranks_ref, sems
-):
-    del after
-    tiles_row, tiles_col, _, rank_cap, _ = u_ref.shape[1:]
-    rank_copy = pltpu.make_async_copy(ranks_hbm, ranks_ref, sems.at[0])
-    v_copy = pltpu.make_async_copy(v_hbm, v_ref, sems.at[1])
-    u_copy = pltpu.make_async_copy(u_hbm, u_ref, sems.at[2])
-    rank_copy.start()
-    v_copy.start()
-    u_copy.start()
     rank_copy.wait()
     lane = lax.broadcasted_iota(jnp.int32, (1, LANES), 1)
     rank = lane % rank_cap
@@ -105,6 +105,25 @@
             cap = jnp.where(low, ranks_ref[b, a], ranks_ref[b, a + 1])
             lanes = slice(a * 2 * rank_cap, (a + 2) * 2 * rank_cap)
             by_col_ref[b : b + 1, lanes] = jnp.where(rank < cap, 1.0, 0.0)
+
+    group = halves * 2 * sources
+    for copy in copies:
+        copy.wait()
+    spectra = (
+        contract_last(basis_ref[...], held[...].reshape(sources * halves * LANES, trace_len))
+        * scale
+    )
+    for g in range(sources):
+        for h in range(halves):
+            lanes = slice((g * halves + h) * LANES, (g * halves + h + 1) * LANES)
+            for c in range(2):
+                rows[pl.ds((h * 2 + c) * sources + g, freq_count, stride=group), :] = spectra[
+                    c * freq_count : (c + 1) * freq_count, lanes
+                ]
+    for f in range(freq_count):
+        piece = rows[f * group : (f + 1) * group, :].astype(jnp.bfloat16)
+        for r in range(copies_out):
+            out_ref[f * copies_out + r] = piece
     v_copy.wait()
     u_copy.wait()
 
@@ -309,8 +328,9 @@
         copy.wait()
 
 
-def spectrum_chunks(traces, freq_count, row_shards):
+def spectrum_chunks(traces, u_bases, v_bases, ranks, freq_count, row_shards):
     sources, _, positions, trace_len = traces.shape
+    tiles_row, tiles_col, _, rank_cap, _ = u_bases.shape[1:]
     halves = positions // LANES
     group = halves * 2 * sources
     return pl.pallas_call(
@@ -318,40 +338,25 @@
         out_shape=(
             jax.ShapeDtypeStruct((freq_count * row_shards, group, LANES), jnp.bfloat16),
             jax.ShapeDtypeStruct((2 * freq_count, trace_len), jnp.bfloat16),
-        ),
-        in_specs=[hbm_spec()],
-        out_specs=(vmem_spec(), vmem_spec()),
-        scratch_shapes=[
-            pltpu.VMEM((sources * halves, LANES, trace_len), jnp.bfloat16),
-            pltpu.VMEM((freq_count * group, LANES), jnp.float32),
-            pltpu.SemaphoreType.DMA((sources * halves,)),
-        ],
-        compiler_params=params(VMEM_MOST),
-        cost_estimate=cost(2 * 2 * freq_count * traces.size, 2 * traces.size),
-        name="spectrum",
-    )(traces)
-
-
-def fetched(u_bases, v_bases, ranks, after):
-    tiles_row, tiles_col, _, rank_cap, _ = u_bases.shape[1:]
-    return pl.pallas_call(
-        fetch_kernel,
-        out_shape=(
             jax.ShapeDtypeStruct(u_bases.shape, jnp.bfloat16),
             jax.ShapeDtypeStruct(v_bases.shape, jnp.bfloat16),
             jax.ShapeDtypeStruct((tiles_row, tiles_col * 2 * rank_cap), jnp.float32),
             jax.ShapeDtypeStruct((tiles_col, tiles_row * 2 * rank_cap), jnp.float32),
         ),
         in_specs=[hbm_spec()] * 4,
-        out_specs=(vmem_spec(),) * 4,
+        out_specs=(vmem_spec(),) * 6,
         scratch_shapes=[
+            pltpu.VMEM((sources * halves, LANES, trace_len), jnp.bfloat16),
+            pltpu.VMEM((freq_count * group, LANES), jnp.float32),
             pltpu.SMEM((tiles_col, tiles_row), jnp.int32),
-            pltpu.SemaphoreType.DMA((3,)),
+            pltpu.SemaphoreType.DMA((3 + sources * halves,)),
         ],
-        compiler_params=params(VMEM_FETCH),
-        cost_estimate=cost(0, 4 * u_bases.size),
-        name="fetch",
-    )(u_bases, v_bases, ranks, after)
+        compiler_params=params(),
+        cost_estimate=cost(
+            2 * 2 * freq_count * traces.size, 2 * (traces.size + 2 * u_bases.size + 2 * v_bases.size)
+        ),
+        name="spectrum",
+    )(in_hbm(traces), in_hbm(u_bases), in_hbm(v_bases), in_hbm(ranks))
 
 
 def forward_chunks(spectra, v_bases, u_bases, mask, virtual):
@@ -440,8 +445,9 @@
     def exchange(chunks, axes):
         return lax.all_to_all(chunks, axes, split_axis=0, concat_axis=0, tiled=True)
 
-    spectra, basis = spectrum_chunks(traces, freq_count, row_shards)
-    u_held, v_held, by_row, by_col = fetched(u_bases, v_bases, ranks[0].T, spectra)
+    spectra, basis, u_held, v_held, by_row, by_col = spectrum_chunks(
+        traces, u_bases, v_bases, ranks[0].T, freq_count, row_shards
+    )
     spectra = exchange(spectra, ("freq", "trow"))
     terms = exchange(forward_chunks(spectra, v_held, u_held, by_col, virtual), "tcol")
     total = exchange(summed_chunks(terms, sources), "tcol")

time: 71.2 us -> 70.2 us (0.986)
  blocking collectives: 42.2 us -> 64.5 us
  starting transfers between devices: 13.9 us -> 0 us
  waiting for transfers between devices: 6.94 us -> 0 us
  local copies, waits for them, and re-layouts: 1.25 us -> 0.01 us
  Pallas kernels: 5.78 us -> 4.75 us
    all_to_all x3 -> x4, blocking collectives: 42.2 us -> 64.5 us  [exchange(): return lax.all_to_all(chunks, axes, split_axis=0, concat_axis=0, tiled=True)]
    all_to_all x1 -> x0, starting transfers between devices: 13.9 us -> none  [exchange(): return lax.all_to_all(chunks, axes, split_axis=0, concat_axis=0, tiled=True)]
    all_to_all x1 -> x0, waiting for transfers between devices: 6.94 us -> none  [exchange(): return lax.all_to_all(chunks, axes, split_axis=0, concat_axis=0, tiled=True)]
    unnamed x12 -> x2, local copies, waits for them, and re-layouts: 1.25 us -> 0.01 us
  transfers between devices with their start and end apart: 1 -> 0, of which waited for: 1 -> 0; matrix products, arithmetic and copies ran while one was open for 0% -> 0% of each run, Pallas kernels for 1% -> 0%
where the time goes in v4:
time: 70.2 us; the launch traced here: 69.9 us
  blocking collectives  64.5 us (92%)
  Pallas kernels  4.75 us (7%)
    all_to_all x4, blocking collectives, exchange(): return lax.all_to_all(chunks, axes, split_axis=0, concat_axis=0, tiled=True)  64.5 us
    pallas_call x1, Pallas kernels, spectrum_chunks(): pl.pallas_call(lambda *refs: spectrum_kernel(1.0 / math.sqrt(trace_len),...  1.93 us

profile of v4, /device:TPU:1, one launch (start us, length us, event | category | flops | bytes accessed | tf_op | source)
XLA Modules:
  0.0 69.9 jit_solution(2326747208535817751)
XLA Ops:
  0.6 1.9 %spectrum.1 = (bf16[32,8,128]{2,1,0:T(8,128)(2,1)S(1)}, bf16[16,1024]{1,0:T(8,128)(2,1)S(1)}, bf16[1,8,4,2,32,256]{5,4,3,2,1,0:T(8,128)(2,1)S(1)}, bf16[1,8,4,2,...) custom-call(bf16[2,1,256,1024]{3,2,1,0:T(8,128)(2,1)} %refs_0_.2, ...), custom_call_target="tpu_custom_call" | custom-call | flops 16777216 | bytes 5242880 | tf_op jit(solution)/shard_map/spectrum/pallas_call | solution.py:336
  2.6 22.3 %all_to_all.20.spec_ref = bf16[32,8,128]{2,1,0:T(8,128)(2,1)S(1)} all-to-all(bf16[32,8,128]{2,1,0:T(8,128)(2,1)S(1)} %get-tuple-element.10), channel_id=1, replica_groups=mesh['freq'=8,'trow'=4,'tcol'=16] {'freq','trow'}, dimensions={0} | all-to-all | bytes 131072 | tf_op jit(solution)/shard_map/all_to_all | solution.py:446
  24.9 0.7 %forward.1 = bf16[16,32,128]{2,1,0:T(8,128)(2,1)S(1)} custom-call(bf16[32,8,128]{2,1,0:T(8,128)(2,1)S(1)} %all_to_all.20.spec_ref, bf16[1,8,4,2,32,256]{5,4,3,2,1,0:T(8,128)(2,1)S(1)} %get-tuple-element.11.v_ref.refs_3_, bf16[1,8,4,2,32,256]{5,4,3,2,1,0:T(8,128)(2,1)S(1)} %get-tuple-element.12.u_ref.refs_2_, f32[4,512]{1,0:T(4,128)S(1)} %get-tuple-element.13.mask_ref), custom_call_target="tpu_custom_call" | custom-call | flops 67108864 | bytes 2097152 | tf_op jit(solution)/shard_map/forward/pallas_call | solution.py:364
  25.6 18.2 %all_to_all.21.refs_0_ = bf16[16,32,128]{2,1,0:T(8,128)(2,1)S(1)} all-to-all(bf16[16,32,128]{2,1,0:T(8,128)(2,1)S(1)} %forward.1), channel_id=1, replica_groups=mesh['freq'=8,'trow'=4,'tcol'=16] {'tcol'}, dimensions={0} | all-to-all | bytes 262144 | tf_op jit(solution)/shard_map/all_to_all | solution.py:446
  43.8 0.0 copy-start
  43.9 11.7 %all_to_all.22.refs_1_ = bf16[16,32,128]{2,1,0:T(8,128)(2,1)S(1)} all-to-all(bf16[16,32,128]{2,1,0:T(8,128)(2,1)S(1)} %total.1), channel_id=1, replica_groups=mesh['freq'=8,'trow'=4,'tcol'=16] {'tcol'}, dimensions={0} | all-to-all | bytes 262144 | tf_op jit(solution)/shard_map/all_to_all | solution.py:446
  55.6 0.0 copy-done
  55.6 0.8 %adjoint.1 = (f32[1,2,16,2048]{3,2,1,0:T(8,128)S(1)}, bf16[32,8,128]{2,1,0:T(8,128)(2,1)S(1)}) custom-call(f32[1,2,16,2048]{3,2,1,0:T(8,128)S(1)} %copy-done, bf16[16,32,128]{2,1,0:T(8,128)(2,1)S(1)} %all_to_all.22.refs_1_, bf16[1,8,4,2,32,256]{5,4,3,2,1,0:T(8,128)(2,1)S(1)} %get-tuple-element.12.u_ref.refs_2_, ...), custom_call_target="tpu_custom_call" | custom-call | flops 67108864 | bytes 2097152 | tf_op jit(solution)/shard_map/adjoint/pallas_call | solution.py:397
  56.4 12.3 %all_to_all.23.refs_1_ = bf16[32,8,128]{2,1,0:T(8,128)(2,1)S(1)} all-to-all(bf16[32,8,128]{2,1,0:T(8,128)(2,1)S(1)} %get-tuple-element.16), channel_id=1, replica_groups=mesh['freq'=8,'trow'=4,'tcol'=16] {'freq','trow'}, dimensions={0} | all-to-all | bytes 131072 | tf_op jit(solution)/shard_map/all_to_all | solution.py:446
  68.6 1.3 %back.1 = (f32[1,2,16,2048]{3,2,1,0:T(8,128)}, bf16[2,1,256,1024]{3,2,1,0:T(8,128)(2,1)}) custom-call(f32[1,2,16,2048]{3,2,1,0:T(8,128)S(1)} %get-tuple-element.15.refs_0_, bf16[32,8,128]{2,1,0:T(8,128)(2,1)S(1)} %all_to_all.23.refs_1_, bf16[16,1024]{1,0:T(8,128)(2,1)S(1)} %get-tuple-element.17.refs_2_), custom_call_target="tpu_custom_call" | custom-call | flops 16777216 | bytes 1048576 | tf_op jit(solution)/shard_map/back/pallas_call | solution.py:420
  (1 shorter events, 0.0 us)
Async XLA Ops:
  43.8 11.8 %copy-start = (f32[1,2,16,2048]{3,2,1,0:T(8,128)S(1)}, f32[1,2,16,2048]{3,2,1,0:T(8,128)}, u32[]{:S(2)}) copy-start(f32[1,2,16,2048]{3,2,1,0:T(8,128)} %refs_0_.3) | copy-start | bytes 786436

commit v5 on v4

--- a/solution.py
+++ b/solution.py
@@ -32,6 +32,20 @@
     return pl.BlockSpec(memory_space=pltpu.HBM)
 
 
+def turned(count, first):
+    return [(first + i) % count for i in range(count)]
+
+
+def exchange_orders(freq_shards, row_shards, col_shards):
+    blocks = [
+        f * row_shards + r
+        for f in turned(freq_shards, freq_shards - 1)
+        for r in turned(row_shards, row_shards - 1)
+    ]
+    columns = [2 * y + core for core in (1, 0) for y in turned(col_shards // 2, col_shards // 4)]
+    return blocks, columns
+
+
 def in_hbm(array):
     return pltpu.with_memory_space_constraint(array, pltpu.HBM)
 
@@ -46,7 +60,7 @@
 
 def spectrum_kernel(
     scale,
-    copies_out,
+    order,
     traces_hbm,
     u_hbm,
     v_hbm,
@@ -120,10 +134,11 @@
                 rows[pl.ds((h * 2 + c) * sources + g, freq_count, stride=group), :] = spectra[
                     c * freq_count : (c + 1) * freq_count, lanes
                 ]
+    copies_out = len(order) // freq_count
     for f in range(freq_count):
         piece = rows[f * group : (f + 1) * group, :].astype(jnp.bfloat16)
         for r in range(copies_out):
-            out_ref[f * copies_out + r] = piece
+            out_ref[order.index(f * copies_out + r)] = piece
     v_copy.wait()
     u_copy.wait()
 
@@ -142,14 +157,14 @@
     return jnp.concatenate([new_top, new_bottom], axis=0).astype(jnp.bfloat16)
 
 
-def forward_kernel(spec_ref, v_ref, u_ref, mask_ref, out_ref, rows):
+def forward_kernel(order, spec_ref, v_ref, u_ref, mask_ref, out_ref, rows):
     chunks, group, _ = spec_ref.shape
     tiles_row, tiles_col, _, rank_cap, tile_len = v_ref.shape[1:]
     owners = chunks // tiles_col
     sources = group // 4
     virtual = owners * sources
     for n in range(chunks):
-        rows[n * group : (n + 1) * group, :] = spec_ref[n].astype(jnp.float32)
+        rows[order[n] * group : (order[n] + 1) * group, :] = spec_ref[n].astype(jnp.float32)
     products = []
     for b in range(tiles_col):
         spectra = jnp.concatenate(
@@ -220,6 +235,7 @@
 
 def adjoint_kernel(
     sources,
+    order,
     observed_ref,
     total_ref,
     u_ref,
@@ -283,13 +299,13 @@
                         :,
                     ] = rows[h, pl.ds((b * 2 + c) * virtual + g, owners, stride=sources), :]
     for n in range(chunks):
-        out_ref[n] = ordered[n * group : (n + 1) * group, :].astype(jnp.bfloat16)
+        out_ref[n] = ordered[order[n] * group : (order[n] + 1) * group, :].astype(jnp.bfloat16)
     for copy in copies:
         copy.wait()
 
 
 def back_kernel(
-    scale, copies_in, residual_ref, parts_ref, basis_ref, residual_hbm, out_hbm, rows, held, sems
+    scale, order, copies_in, residual_ref, parts_ref, basis_ref, residual_hbm, out_hbm, rows, held, sems
 ):
     pieces = held.shape[0]
     kept = pltpu.make_async_copy(residual_ref, residual_hbm, sems.at[pieces])
@@ -298,9 +314,9 @@
     freq_count = chunks // copies_in
     sources = group // 4
     for f in range(freq_count):
-        total = parts_ref[f * copies_in].astype(jnp.float32)
+        total = parts_ref[order.index(f * copies_in)].astype(jnp.float32)
         for r in range(1, copies_in):
-            total = total + parts_ref[f * copies_in + r].astype(jnp.float32)
+            total = total + parts_ref[order.index(f * copies_in + r)].astype(jnp.float32)
         rows[f * group : (f + 1) * group, :] = total
     basis = basis_ref[...]
     copies = [kept]
@@ -328,15 +344,15 @@
         copy.wait()
 
 
-def spectrum_chunks(traces, u_bases, v_bases, ranks, freq_count, row_shards):
+def spectrum_chunks(traces, u_bases, v_bases, ranks, freq_count, order):
     sources, _, positions, trace_len = traces.shape
     tiles_row, tiles_col, _, rank_cap, _ = u_bases.shape[1:]
     halves = positions // LANES
     group = halves * 2 * sources
     return pl.pallas_call(
-        lambda *refs: spectrum_kernel(1.0 / math.sqrt(trace_len), row_shards, *refs),
+        lambda *refs: spectrum_kernel(1.0 / math.sqrt(trace_len), order, *refs),
         out_shape=(
-            jax.ShapeDtypeStruct((freq_count * row_shards, group, LANES), jnp.bfloat16),
+            jax.ShapeDtypeStruct((len(order), group, LANES), jnp.bfloat16),
             jax.ShapeDtypeStruct((2 * freq_count, trace_len), jnp.bfloat16),
             jax.ShapeDtypeStruct(u_bases.shape, jnp.bfloat16),
             jax.ShapeDtypeStruct(v_bases.shape, jnp.bfloat16),
@@ -359,10 +375,10 @@
     )(in_hbm(traces), in_hbm(u_bases), in_hbm(v_bases), in_hbm(ranks))
 
 
-def forward_chunks(spectra, v_bases, u_bases, mask, virtual):
+def forward_chunks(spectra, v_bases, u_bases, mask, virtual, order):
     tiles_row = u_bases.shape[1]
     return pl.pallas_call(
-        forward_kernel,
+        lambda *refs: forward_kernel(order, *refs),
         out_shape=jax.ShapeDtypeStruct((2 * tiles_row, 2 * virtual, LANES), jnp.bfloat16),
         in_specs=[vmem_spec()] * 4,
         out_specs=vmem_spec(),
@@ -388,14 +404,14 @@
     )(parts)
 
 
-def adjoint_chunks(observed, total, u_bases, v_bases, mask, sources):
+def adjoint_chunks(observed, total, u_bases, v_bases, mask, sources, order):
     tiles_col = u_bases.shape[2]
     tile_len = u_bases.shape[5]
     virtual = observed.shape[2]
     group = 4 * sources
     chunks = tiles_col * virtual // sources
     return pl.pallas_call(
-        lambda *refs: adjoint_kernel(sources, *refs),
+        lambda *refs: adjoint_kernel(sources, order, *refs),
         out_shape=(
             jax.ShapeDtypeStruct(observed.shape, jnp.float32),
             jax.ShapeDtypeStruct((chunks, group, LANES), jnp.bfloat16),
@@ -413,12 +429,12 @@
     )(observed, total, u_bases, v_bases, mask)
 
 
-def back_traces(residual, parts, basis, row_shards, shape):
+def back_traces(residual, parts, basis, row_shards, shape, order):
     freq_count = basis.shape[0] // 2
     group = parts.shape[1]
     pieces = shape[0] * shape[2] // LANES
     return pl.pallas_call(
-        lambda *refs: back_kernel(1.0 / math.sqrt(freq_count), row_shards, *refs),
+        lambda *refs: back_kernel(1.0 / math.sqrt(freq_count), order, row_shards, *refs),
         out_shape=(
             jax.ShapeDtypeStruct(residual.shape, jnp.float32),
             jax.ShapeDtypeStruct(shape, jnp.bfloat16),
@@ -442,18 +458,23 @@
     freq_count = u_bases.shape[0] * lax.axis_size("freq")
     row_shards = lax.axis_size("trow")
 
-    def exchange(chunks, axes):
-        return lax.all_to_all(chunks, axes, split_axis=0, concat_axis=0, tiled=True)
+    blocks, columns = exchange_orders(lax.axis_size("freq"), row_shards, lax.axis_size("tcol"))
+
+    def exchange(chunks, axes, order):
+        return lax.all_to_all(
+            chunks, axes, split_axis=0, concat_axis=0, tiled=True, axis_index_groups=[order]
+        )
 
     spectra, basis, u_held, v_held, by_row, by_col = spectrum_chunks(
-        traces, u_bases, v_bases, ranks[0].T, freq_count, row_shards
-    )
-    spectra = exchange(spectra, ("freq", "trow"))
-    terms = exchange(forward_chunks(spectra, v_held, u_held, by_col, virtual), "tcol")
-    total = exchange(summed_chunks(terms, sources), "tcol")
-    residual, back = adjoint_chunks(observed, total, u_held, v_held, by_row, sources)
-    back = exchange(back, ("freq", "trow"))
-    return back_traces(residual, back, basis, row_shards, traces.shape)
+        traces, u_bases, v_bases, ranks[0].T, freq_count, blocks
+    )
+    spectra = exchange(spectra, ("freq", "trow"), blocks)
+    terms = forward_chunks(spectra, v_held, u_held, by_col, virtual, blocks)
+    terms = exchange(terms, "tcol", columns)
+    total = exchange(summed_chunks(terms, sources), "tcol", columns)
+    residual, back = adjoint_chunks(observed, total, u_held, v_held, by_row, sources, blocks)
+    back = exchange(back, ("freq", "trow"), blocks)
+    return back_traces(residual, back, basis, row_shards, traces.shape, blocks)
 
 
 def solution(mesh):

time: 70.2 us -> 62.3 us (0.89)
  blocking collectives: 64.5 us -> 56.5 us
    all_to_all x4, blocking collectives: 64.5 us -> 56.5 us  [exchange(): lax.all_to_all(chunks, axes, split_axis=0, concat_axis=0, tiled=True, axi...]
where the time goes in v5:
time: 62.3 us; the launch traced here: 61.9 us
  blocking collectives  56.5 us (91%)
  Pallas kernels  4.76 us (8%)
  between operations  0.66 us (1%)
    all_to_all x4, blocking collectives, exchange(): lax.all_to_all(chunks, axes, split_axis=0, concat_axis=0, tiled=True, axi...  56.5 us
    pallas_call x1, Pallas kernels, spectrum_chunks(): pl.pallas_call(lambda *refs: spectrum_kernel(1.0 / math.sqrt(trace_len),...  1.93 us
    pallas_call x1, Pallas kernels, back_traces(): pl.pallas_call(lambda *refs: back_kernel(1.0 / math.sqrt(freq_count), ord...  1.28 us

profile of v5, /device:TPU:1, one launch (start us, length us, event | category | flops | bytes accessed | tf_op | source)
XLA Modules:
  0.0 61.9 jit_solution(13447038444362912506)
XLA Ops:
  0.6 1.9 %spectrum.1 = (bf16[32,8,128]{2,1,0:T(8,128)(2,1)S(1)}, bf16[16,1024]{1,0:T(8,128)(2,1)S(1)}, bf16[1,8,4,2,32,256]{5,4,3,2,1,0:T(8,128)(2,1)S(1)}, bf16[1,8,4,2,...) custom-call(bf16[2,1,256,1024]{3,2,1,0:T(8,128)(2,1)} %refs_0_.2, ...), custom_call_target="tpu_custom_call" | custom-call | flops 16777216 | bytes 5242880 | tf_op jit(solution)/shard_map/spectrum/pallas_call | solution.py:352
  2.6 20.2 %all_to_all.20.refs_0_ = bf16[32,8,128]{2,1,0:T(8,128)(2,1)S(1)} all-to-all(bf16[32,8,128]{2,1,0:T(8,128)(2,1)S(1)} %get-tuple-element.10), channel_id=1, replica_groups={{496,448,464,480,48,0,16,32,112,64,80,96,176,128,144,160,240,192,208,22..., dimensions={0} | all-to-all | bytes 131072 | tf_op jit(solution)/shard_map/all_to_all | solution.py:464
  22.7 0.7 %forward.1 = bf16[16,32,128]{2,1,0:T(8,128)(2,1)S(1)} custom-call(bf16[32,8,128]{2,1,0:T(8,128)(2,1)S(1)} %all_to_all.20.refs_0_, bf16[1,8,4,2,32,256]{5,4,3,2,1,0:T(8,128)(2,1)S(1)} %get-tuple-element.11.refs_1_.refs_3_, bf16[1,8,4,2,32,256]{5,4,3,2,1,0:T(8,128)(2,1)S(1)} %get-tuple-element.12.refs_2_, f32[4,512]{1,0:T(4,128)S(1)} %get-tuple-element.13.refs_3_), custom_call_target="tpu_custom_call" | custom-call | flops 67108864 | bytes 2097152 | tf_op jit(solution)/shard_map/forward/pallas_call | solution.py:380
  23.5 13.0 %all_to_all.21.refs_0_ = bf16[16,32,128]{2,1,0:T(8,128)(2,1)S(1)} all-to-all(bf16[16,32,128]{2,1,0:T(8,128)(2,1)S(1)} %forward.1), channel_id=1, replica_groups={{9,11,13,15,1,3,5,7,8,10,12,14,0,2,4,6},{25,27,29,31,17,19,21,23,24,26,..., dimensions={0} | all-to-all | bytes 262144 | tf_op jit(solution)/shard_map/all_to_all | solution.py:464
  36.5 0.0 copy-start
  36.5 11.3 %all_to_all.22.refs_1_ = bf16[16,32,128]{2,1,0:T(8,128)(2,1)S(1)} all-to-all(bf16[16,32,128]{2,1,0:T(8,128)(2,1)S(1)} %total.1), channel_id=1, replica_groups={{9,11,13,15,1,3,5,7,8,10,12,14,0,2,4,6},{25,27,29,31,17,19,21,23,24,26,..., dimensions={0} | all-to-all | bytes 262144 | tf_op jit(solution)/shard_map/all_to_all | solution.py:464
  47.9 0.0 copy-done
  47.9 0.8 %adjoint.1 = (f32[1,2,16,2048]{3,2,1,0:T(8,128)S(1)}, bf16[32,8,128]{2,1,0:T(8,128)(2,1)S(1)}) custom-call(f32[1,2,16,2048]{3,2,1,0:T(8,128)S(1)} %copy-done, bf16[16,32,128]{2,1,0:T(8,128)(2,1)S(1)} %all_to_all.22.refs_1_, bf16[1,8,4,2,32,256]{5,4,3,2,1,0:T(8,128)(2,1)S(1)} %get-tuple-element.12.refs_2_, ...), custom_call_target="tpu_custom_call" | custom-call | flops 67108864 | bytes 2097152 | tf_op jit(solution)/shard_map/adjoint/pallas_call | solution.py:413
  48.7 12.0 %all_to_all.23.refs_1_ = bf16[32,8,128]{2,1,0:T(8,128)(2,1)S(1)} all-to-all(bf16[32,8,128]{2,1,0:T(8,128)(2,1)S(1)} %get-tuple-element.16), channel_id=1, replica_groups={{496,448,464,480,48,0,16,32,112,64,80,96,176,128,144,160,240,192,208,22..., dimensions={0} | all-to-all | bytes 131072 | tf_op jit(solution)/shard_map/all_to_all | solution.py:464
  60.6 1.3 %back.1 = (f32[1,2,16,2048]{3,2,1,0:T(8,128)}, bf16[2,1,256,1024]{3,2,1,0:T(8,128)(2,1)}) custom-call(f32[1,2,16,2048]{3,2,1,0:T(8,128)S(1)} %get-tuple-element.15.refs_0_, bf16[32,8,128]{2,1,0:T(8,128)(2,1)S(1)} %all_to_all.23.refs_1_, bf16[16,1024]{1,0:T(8,128)(2,1)S(1)} %get-tuple-element.17.refs_2_), custom_call_target="tpu_custom_call" | custom-call | flops 16777216 | bytes 1048576 | tf_op jit(solution)/shard_map/back/pallas_call | solution.py:436
  (1 shorter events, 0.0 us)
Async XLA Ops:
  36.5 11.4 %copy-start = (f32[1,2,16,2048]{3,2,1,0:T(8,128)S(1)}, f32[1,2,16,2048]{3,2,1,0:T(8,128)}, u32[]{:S(2)}) copy-start(f32[1,2,16,2048]{3,2,1,0:T(8,128)} %refs_0_.3) | copy-start | bytes 786436

commit v6 on v5

--- a/solution.py
+++ b/solution.py
@@ -37,13 +37,15 @@
 
 
 def exchange_orders(freq_shards, row_shards, col_shards):
-    blocks = [
-        f * row_shards + r
-        for f in turned(freq_shards, freq_shards - 1)
-        for r in turned(row_shards, row_shards - 1)
-    ]
+    def blocks(first_row):
+        return [
+            f * row_shards + r
+            for f in turned(freq_shards, freq_shards - 1)
+            for r in turned(row_shards, first_row)
+        ]
+
     columns = [2 * y + core for core in (1, 0) for y in turned(col_shards // 2, col_shards // 4)]
-    return blocks, columns
+    return blocks(row_shards - 1), columns, blocks(row_shards // 2)
 
 
 def in_hbm(array):
@@ -458,7 +460,7 @@
     freq_count = u_bases.shape[0] * lax.axis_size("freq")
     row_shards = lax.axis_size("trow")
 
-    blocks, columns = exchange_orders(lax.axis_size("freq"), row_shards, lax.axis_size("tcol"))
+    outward, columns, homeward = exchange_orders(lax.axis_size("freq"), row_shards, lax.axis_size("tcol"))
 
     def exchange(chunks, axes, order):
         return lax.all_to_all(
@@ -466,15 +468,15 @@
         )
 
     spectra, basis, u_held, v_held, by_row, by_col = spectrum_chunks(
-        traces, u_bases, v_bases, ranks[0].T, freq_count, blocks
-    )
-    spectra = exchange(spectra, ("freq", "trow"), blocks)
-    terms = forward_chunks(spectra, v_held, u_held, by_col, virtual, blocks)
+        traces, u_bases, v_bases, ranks[0].T, freq_count, outward
+    )
+    spectra = exchange(spectra, ("freq", "trow"), outward)
+    terms = forward_chunks(spectra, v_held, u_held, by_col, virtual, outward)
     terms = exchange(terms, "tcol", columns)
     total = exchange(summed_chunks(terms, sources), "tcol", columns)
-    residual, back = adjoint_chunks(observed, total, u_held, v_held, by_row, sources, blocks)
-    back = exchange(back, ("freq", "trow"), blocks)
-    return back_traces(residual, back, basis, row_shards, traces.shape, blocks)
+    residual, back = adjoint_chunks(observed, total, u_held, v_held, by_row, sources, homeward)
+    back = exchange(back, ("freq", "trow"), homeward)
+    return back_traces(residual, back, basis, row_shards, traces.shape, homeward)
 
 
 def solution(mesh):

time: 62.3 us -> 61.9 us (level)
  no operation moved by 1% of the time
where the time goes in v6:
time: 61.9 us; the launch traced here: 61.5 us
  blocking collectives  56.1 us (91%)
  Pallas kernels  4.77 us (8%)
  between operations  0.66 us (1%)
    all_to_all x4, blocking collectives, exchange(): lax.all_to_all(chunks, axes, split_axis=0, concat_axis=0, tiled=True, axi...  56.1 us
    pallas_call x1, Pallas kernels, spectrum_chunks(): pl.pallas_call(lambda *refs: spectrum_kernel(1.0 / math.sqrt(trace_len),...  1.93 us
    pallas_call x1, Pallas kernels, back_traces(): pl.pallas_call(lambda *refs: back_kernel(1.0 / math.sqrt(freq_count), ord...  1.28 us

profile of v6, /device:TPU:1, one launch (start us, length us, event | category | flops | bytes accessed | tf_op | source)
XLA Modules:
  0.0 61.5 jit_solution(4377036692835635460)
XLA Ops:
  0.6 1.9 %spectrum.1 = (bf16[32,8,128]{2,1,0:T(8,128)(2,1)S(1)}, bf16[16,1024]{1,0:T(8,128)(2,1)S(1)}, bf16[1,8,4,2,32,256]{5,4,3,2,1,0:T(8,128)(2,1)S(1)}, bf16[1,8,4,2,...) custom-call(bf16[2,1,256,1024]{3,2,1,0:T(8,128)(2,1)} %refs_0_.2, ...), custom_call_target="tpu_custom_call" | custom-call | flops 16777216 | bytes 5242880 | tf_op jit(solution)/shard_map/spectrum/pallas_call | solution.py:354
  2.6 20.2 %all_to_all.20.refs_0_ = bf16[32,8,128]{2,1,0:T(8,128)(2,1)S(1)} all-to-all(bf16[32,8,128]{2,1,0:T(8,128)(2,1)S(1)} %get-tuple-element.10), channel_id=1, replica_groups={{496,448,464,480,48,0,16,32,112,64,80,96,176,128,144,160,240,192,208,22..., dimensions={0} | all-to-all | bytes 131072 | tf_op jit(solution)/shard_map/all_to_all | solution.py:466
  22.7 0.7 %forward.1 = bf16[16,32,128]{2,1,0:T(8,128)(2,1)S(1)} custom-call(bf16[32,8,128]{2,1,0:T(8,128)(2,1)S(1)} %all_to_all.20.refs_0_, bf16[1,8,4,2,32,256]{5,4,3,2,1,0:T(8,128)(2,1)S(1)} %get-tuple-element.11.refs_1_.refs_3_, bf16[1,8,4,2,32,256]{5,4,3,2,1,0:T(8,128)(2,1)S(1)} %get-tuple-element.12.refs_2_, f32[4,512]{1,0:T(4,128)S(1)} %get-tuple-element.13.refs_3_), custom_call_target="tpu_custom_call" | custom-call | flops 67108864 | bytes 2097152 | tf_op jit(solution)/shard_map/forward/pallas_call | solution.py:382
  23.5 13.0 %all_to_all.21.refs_0_ = bf16[16,32,128]{2,1,0:T(8,128)(2,1)S(1)} all-to-all(bf16[16,32,128]{2,1,0:T(8,128)(2,1)S(1)} %forward.1), channel_id=1, replica_groups={{9,11,13,15,1,3,5,7,8,10,12,14,0,2,4,6},{25,27,29,31,17,19,21,23,24,26,..., dimensions={0} | all-to-all | bytes 262144 | tf_op jit(solution)/shard_map/all_to_all | solution.py:466
  36.5 0.0 copy-start
  36.5 11.3 %all_to_all.22.refs_1_ = bf16[16,32,128]{2,1,0:T(8,128)(2,1)S(1)} all-to-all(bf16[16,32,128]{2,1,0:T(8,128)(2,1)S(1)} %total.1), channel_id=1, replica_groups={{9,11,13,15,1,3,5,7,8,10,12,14,0,2,4,6},{25,27,29,31,17,19,21,23,24,26,..., dimensions={0} | all-to-all | bytes 262144 | tf_op jit(solution)/shard_map/all_to_all | solution.py:466
  47.9 0.0 copy-done
  47.9 0.8 %adjoint.1 = (f32[1,2,16,2048]{3,2,1,0:T(8,128)S(1)}, bf16[32,8,128]{2,1,0:T(8,128)(2,1)S(1)}) custom-call(f32[1,2,16,2048]{3,2,1,0:T(8,128)S(1)} %copy-done, bf16[16,32,128]{2,1,0:T(8,128)(2,1)S(1)} %all_to_all.22.refs_1_, bf16[1,8,4,2,32,256]{5,4,3,2,1,0:T(8,128)(2,1)S(1)} %get-tuple-element.12.refs_2_, ...), custom_call_target="tpu_custom_call" | custom-call | flops 67108864 | bytes 2097152 | tf_op jit(solution)/shard_map/adjoint/pallas_call | solution.py:415
  48.7 11.6 %all_to_all.23.refs_1_ = bf16[32,8,128]{2,1,0:T(8,128)(2,1)S(1)} all-to-all(bf16[32,8,128]{2,1,0:T(8,128)(2,1)S(1)} %get-tuple-element.16), channel_id=1, replica_groups={{480,496,448,464,32,48,0,16,96,112,64,80,160,176,128,144,224,240,192,20..., dimensions={0} | all-to-all | bytes 131072 | tf_op jit(solution)/shard_map/all_to_all | solution.py:466
  60.2 1.3 %back.1 = (f32[1,2,16,2048]{3,2,1,0:T(8,128)}, bf16[2,1,256,1024]{3,2,1,0:T(8,128)(2,1)}) custom-call(f32[1,2,16,2048]{3,2,1,0:T(8,128)S(1)} %get-tuple-element.15.refs_0_, bf16[32,8,128]{2,1,0:T(8,128)(2,1)S(1)} %all_to_all.23.refs_1_, bf16[16,1024]{1,0:T(8,128)(2,1)S(1)} %get-tuple-element.17.refs_2_), custom_call_target="tpu_custom_call" | custom-call | flops 16777216 | bytes 1048576 | tf_op jit(solution)/shard_map/back/pallas_call | solution.py:438
  (1 shorter events, 0.0 us)
Async XLA Ops:
  36.5 11.4 %copy-start = (f32[1,2,16,2048]{3,2,1,0:T(8,128)S(1)}, f32[1,2,16,2048]{3,2,1,0:T(8,128)}, u32[]{:S(2)}) copy-start(f32[1,2,16,2048]{3,2,1,0:T(8,128)} %refs_0_.3) | copy-start | bytes 786436

commit v7 on v6

--- a/solution.py
+++ b/solution.py
@@ -230,7 +230,7 @@
         for g in range(sources):
             start = c * virtual + g * owners
             rows[pl.ds(c * virtual + g, owners, stride=sources), :] = total[start : start + owners]
-    piece = rows[...].astype(jnp.bfloat16)
+    piece = rows[:height, :].astype(jnp.bfloat16)
     for n in range(count):
         out_ref[n] = piece
 
@@ -365,7 +365,7 @@
         out_specs=(vmem_spec(),) * 6,
         scratch_shapes=[
             pltpu.VMEM((sources * halves, LANES, trace_len), jnp.bfloat16),
-            pltpu.VMEM((freq_count * group, LANES), jnp.float32),
+            pltpu.VMEM(((freq_count + 1) * group, LANES), jnp.float32),
             pltpu.SMEM((tiles_col, tiles_row), jnp.int32),
             pltpu.SemaphoreType.DMA((3 + sources * halves,)),
         ],
@@ -385,7 +385,7 @@
         in_specs=[vmem_spec()] * 4,
         out_specs=vmem_spec(),
         scratch_shapes=[
-            pltpu.VMEM((spectra.shape[0] * spectra.shape[1], LANES), jnp.float32),
+            pltpu.VMEM(((spectra.shape[0] + v_bases.shape[2]) * spectra.shape[1], LANES), jnp.float32),
         ],
         compiler_params=params(),
         cost_estimate=cost(8 * virtual * u_bases.size, 4 * u_bases.size),
@@ -399,7 +399,7 @@
         out_shape=jax.ShapeDtypeStruct(parts.shape, jnp.bfloat16),
         in_specs=[vmem_spec()],
         out_specs=vmem_spec(),
-        scratch_shapes=[pltpu.VMEM(parts.shape[1:], jnp.float32)],
+        scratch_shapes=[pltpu.VMEM((parts.shape[1] + SUBLANES, LANES), jnp.float32)],
         compiler_params=params(),
         cost_estimate=cost(parts.size, 4 * parts.size),
         name="total",
@@ -421,8 +421,8 @@
         in_specs=[vmem_spec()] * 5,
         out_specs=(vmem_spec(), vmem_spec()),
         scratch_shapes=[
-            pltpu.VMEM((tile_len // LANES, tiles_col * 2 * virtual, LANES), jnp.float32),
-            pltpu.VMEM((chunks * group, LANES), jnp.float32),
+            pltpu.VMEM((tile_len // LANES, tiles_col * 2 * virtual + SUBLANES, LANES), jnp.float32),
+            pltpu.VMEM(((chunks + tiles_col) * group, LANES), jnp.float32),
             pltpu.SemaphoreType.DMA((u_bases.shape[1] // 4,)),
         ],
         compiler_params=params(),
@@ -444,7 +444,7 @@
         in_specs=[vmem_spec()] * 3,
         out_specs=(hbm_spec(), hbm_spec()),
         scratch_shapes=[
-            pltpu.VMEM((freq_count * group, LANES), jnp.float32),
+            pltpu.VMEM(((freq_count + 1) * group, LANES), jnp.float32),
             pltpu.VMEM((pieces, LANES, shape[3]), jnp.bfloat16),
             pltpu.SemaphoreType.DMA((pieces + 1,)),
         ],
@@ -460,7 +460,9 @@
     freq_count = u_bases.shape[0] * lax.axis_size("freq")
     row_shards = lax.axis_size("trow")
 
-    outward, columns, homeward = exchange_orders(lax.axis_size("freq"), row_shards, lax.axis_size("tcol"))
+    outward, columns, homeward = exchange_orders(
+        lax.axis_size("freq"), row_shards, lax.axis_size("tcol")
+    )
 
     def exchange(chunks, axes, order):
         return lax.all_to_all(

time: 61.9 us -> 61.9 us (level)
  no operation moved by 1% of the time
where the time goes in v7:
time: 61.9 us; the launch traced here: 61.5 us
  blocking collectives  56.1 us (91%)
  Pallas kernels  4.76 us (8%)
  between operations  0.66 us (1%)
    all_to_all x4, blocking collectives, exchange(): lax.all_to_all(chunks, axes, split_axis=0, concat_axis=0, tiled=True, axi...  56.1 us
    pallas_call x1, Pallas kernels, spectrum_chunks(): pl.pallas_call(lambda *refs: spectrum_kernel(1.0 / math.sqrt(trace_len),...  1.93 us
    pallas_call x1, Pallas kernels, back_traces(): pl.pallas_call(lambda *refs: back_kernel(1.0 / math.sqrt(freq_count), ord...  1.27 us

profile of v7, /device:TPU:1, one launch (start us, length us, event | category | flops | bytes accessed | tf_op | source)
XLA Modules:
  0.0 61.5 jit_solution(2990519781104721269)
XLA Ops:
  0.6 1.9 %spectrum.1 = (bf16[32,8,128]{2,1,0:T(8,128)(2,1)S(1)}, bf16[16,1024]{1,0:T(8,128)(2,1)S(1)}, bf16[1,8,4,2,32,256]{5,4,3,2,1,0:T(8,128)(2,1)S(1)}, bf16[1,8,4,2,...) custom-call(bf16[2,1,256,1024]{3,2,1,0:T(8,128)(2,1)} %refs_0_.2, ...), custom_call_target="tpu_custom_call" | custom-call | flops 16777216 | bytes 5242880 | tf_op jit(solution)/shard_map/spectrum/pallas_call | solution.py:354
  2.6 20.2 %all_to_all.20.refs_0_ = bf16[32,8,128]{2,1,0:T(8,128)(2,1)S(1)} all-to-all(bf16[32,8,128]{2,1,0:T(8,128)(2,1)S(1)} %get-tuple-element.10), channel_id=1, replica_groups={{496,448,464,480,48,0,16,32,112,64,80,96,176,128,144,160,240,192,208,22..., dimensions={0} | all-to-all | bytes 131072 | tf_op jit(solution)/shard_map/all_to_all | solution.py:468
  22.7 0.7 %forward.1 = bf16[16,32,128]{2,1,0:T(8,128)(2,1)S(1)} custom-call(bf16[32,8,128]{2,1,0:T(8,128)(2,1)S(1)} %all_to_all.20.refs_0_, bf16[1,8,4,2,32,256]{5,4,3,2,1,0:T(8,128)(2,1)S(1)} %get-tuple-element.11.refs_1_.refs_3_, bf16[1,8,4,2,32,256]{5,4,3,2,1,0:T(8,128)(2,1)S(1)} %get-tuple-element.12.refs_2_, f32[4,512]{1,0:T(4,128)S(1)} %get-tuple-element.13.refs_3_), custom_call_target="tpu_custom_call" | custom-call | flops 67108864 | bytes 2097152 | tf_op jit(solution)/shard_map/forward/pallas_call | solution.py:382
  23.5 13.0 %all_to_all.21.refs_0_ = bf16[16,32,128]{2,1,0:T(8,128)(2,1)S(1)} all-to-all(bf16[16,32,128]{2,1,0:T(8,128)(2,1)S(1)} %forward.1), channel_id=1, replica_groups={{9,11,13,15,1,3,5,7,8,10,12,14,0,2,4,6},{25,27,29,31,17,19,21,23,24,26,..., dimensions={0} | all-to-all | bytes 262144 | tf_op jit(solution)/shard_map/all_to_all | solution.py:468
  36.5 0.0 copy-start
  36.5 11.3 %all_to_all.22.refs_1_ = bf16[16,32,128]{2,1,0:T(8,128)(2,1)S(1)} all-to-all(bf16[16,32,128]{2,1,0:T(8,128)(2,1)S(1)} %total.1), channel_id=1, replica_groups={{9,11,13,15,1,3,5,7,8,10,12,14,0,2,4,6},{25,27,29,31,17,19,21,23,24,26,..., dimensions={0} | all-to-all | bytes 262144 | tf_op jit(solution)/shard_map/all_to_all | solution.py:468
  47.9 0.0 copy-done
  47.9 0.8 %adjoint.1 = (f32[1,2,16,2048]{3,2,1,0:T(8,128)S(1)}, bf16[32,8,128]{2,1,0:T(8,128)(2,1)S(1)}) custom-call(f32[1,2,16,2048]{3,2,1,0:T(8,128)S(1)} %copy-done, bf16[16,32,128]{2,1,0:T(8,128)(2,1)S(1)} %all_to_all.22.refs_1_, bf16[1,8,4,2,32,256]{5,4,3,2,1,0:T(8,128)(2,1)S(1)} %get-tuple-element.12.refs_2_, ...), custom_call_target="tpu_custom_call" | custom-call | flops 67108864 | bytes 2097152 | tf_op jit(solution)/shard_map/adjoint/pallas_call | solution.py:415
  48.7 11.6 %all_to_all.23.refs_1_ = bf16[32,8,128]{2,1,0:T(8,128)(2,1)S(1)} all-to-all(bf16[32,8,128]{2,1,0:T(8,128)(2,1)S(1)} %get-tuple-element.16), channel_id=1, replica_groups={{480,496,448,464,32,48,0,16,96,112,64,80,160,176,128,144,224,240,192,20..., dimensions={0} | all-to-all | bytes 131072 | tf_op jit(solution)/shard_map/all_to_all | solution.py:468
  60.2 1.3 %back.1 = (f32[1,2,16,2048]{3,2,1,0:T(8,128)}, bf16[2,1,256,1024]{3,2,1,0:T(8,128)(2,1)}) custom-call(f32[1,2,16,2048]{3,2,1,0:T(8,128)S(1)} %get-tuple-element.15.refs_0_, bf16[32,8,128]{2,1,0:T(8,128)(2,1)S(1)} %all_to_all.23.refs_1_, bf16[16,1024]{1,0:T(8,128)(2,1)S(1)} %get-tuple-element.17.refs_2_), custom_call_target="tpu_custom_call" | custom-call | flops 16777216 | bytes 1048576 | tf_op jit(solution)/shard_map/back/pallas_call | solution.py:438
  (1 shorter events, 0.0 us)
Async XLA Ops:
  36.5 11.4 %copy-start = (f32[1,2,16,2048]{3,2,1,0:T(8,128)S(1)}, f32[1,2,16,2048]{3,2,1,0:T(8,128)}, u32[]{:S(2)}) copy-start(f32[1,2,16,2048]{3,2,1,0:T(8,128)} %refs_0_.3) | copy-start | bytes 786436

commit v8 on v7

--- a/solution.py
+++ b/solution.py
@@ -44,7 +44,8 @@
             for r in turned(row_shards, first_row)
         ]
 
-    columns = [2 * y + core for core in (1, 0) for y in turned(col_shards // 2, col_shards // 4)]
+    chips = col_shards // 2
+    columns = [2 * ((chips // 2 + 3 * i) % chips) + core for core in (1, 0) for i in range(chips)]
     return blocks(row_shards - 1), columns, blocks(row_shards // 2)
 
 

time: 61.9 us -> 61.7 us (level)
  no operation moved by 1% of the time
where the time goes in v8:
time: 61.7 us; the launch traced here: 61.3 us
  blocking collectives  55.9 us (91%)
  Pallas kernels  4.76 us (8%)
  between operations  0.66 us (1%)
    all_to_all x4, blocking collectives, exchange(): lax.all_to_all(chunks, axes, split_axis=0, concat_axis=0, tiled=True, axi...  55.9 us
    pallas_call x1, Pallas kernels, spectrum_chunks(): pl.pallas_call(lambda *refs: spectrum_kernel(1.0 / math.sqrt(trace_len),...  1.93 us
    pallas_call x1, Pallas kernels, back_traces(): pl.pallas_call(lambda *refs: back_kernel(1.0 / math.sqrt(freq_count), ord...  1.28 us

profile of v8, /device:TPU:1, one launch (start us, length us, event | category | flops | bytes accessed | tf_op | source)
XLA Modules:
  0.0 61.3 jit_solution(14971847487983246342)
XLA Ops:
  0.6 1.9 %spectrum.1 = (bf16[32,8,128]{2,1,0:T(8,128)(2,1)S(1)}, bf16[16,1024]{1,0:T(8,128)(2,1)S(1)}, bf16[1,8,4,2,32,256]{5,4,3,2,1,0:T(8,128)(2,1)S(1)}, bf16[1,8,4,2,...) custom-call(bf16[2,1,256,1024]{3,2,1,0:T(8,128)(2,1)} %refs_0_.2, ...), custom_call_target="tpu_custom_call" | custom-call | flops 16777216 | bytes 5242880 | tf_op jit(solution)/shard_map/spectrum/pallas_call | solution.py:355
  2.6 20.2 %all_to_all.20.refs_0_ = bf16[32,8,128]{2,1,0:T(8,128)(2,1)S(1)} all-to-all(bf16[32,8,128]{2,1,0:T(8,128)(2,1)S(1)} %get-tuple-element.10), channel_id=1, replica_groups={{496,448,464,480,48,0,16,32,112,64,80,96,176,128,144,160,240,192,208,22..., dimensions={0} | all-to-all | bytes 131072 | tf_op jit(solution)/shard_map/all_to_all | solution.py:469
  22.7 0.7 %forward.1 = bf16[16,32,128]{2,1,0:T(8,128)(2,1)S(1)} custom-call(bf16[32,8,128]{2,1,0:T(8,128)(2,1)S(1)} %all_to_all.20.refs_0_, bf16[1,8,4,2,32,256]{5,4,3,2,1,0:T(8,128)(2,1)S(1)} %get-tuple-element.11.refs_1_.refs_3_, bf16[1,8,4,2,32,256]{5,4,3,2,1,0:T(8,128)(2,1)S(1)} %get-tuple-element.12.refs_2_, f32[4,512]{1,0:T(4,128)S(1)} %get-tuple-element.13.refs_3_), custom_call_target="tpu_custom_call" | custom-call | flops 67108864 | bytes 2097152 | tf_op jit(solution)/shard_map/forward/pallas_call | solution.py:383
  23.5 12.9 %all_to_all.21.refs_0_ = bf16[16,32,128]{2,1,0:T(8,128)(2,1)S(1)} all-to-all(bf16[16,32,128]{2,1,0:T(8,128)(2,1)S(1)} %forward.1), channel_id=1, replica_groups={{9,15,5,11,1,7,13,3,8,14,4,10,0,6,12,2},{25,31,21,27,17,23,29,19,24,30,..., dimensions={0} | all-to-all | bytes 262144 | tf_op jit(solution)/shard_map/all_to_all | solution.py:469
  36.3 0.0 copy-start
  36.4 11.3 %all_to_all.22.refs_1_ = bf16[16,32,128]{2,1,0:T(8,128)(2,1)S(1)} all-to-all(bf16[16,32,128]{2,1,0:T(8,128)(2,1)S(1)} %total.1), channel_id=1, replica_groups={{9,15,5,11,1,7,13,3,8,14,4,10,0,6,12,2},{25,31,21,27,17,23,29,19,24,30,..., dimensions={0} | all-to-all | bytes 262144 | tf_op jit(solution)/shard_map/all_to_all | solution.py:469
  47.7 0.0 copy-done
  47.7 0.8 %adjoint.1 = (f32[1,2,16,2048]{3,2,1,0:T(8,128)S(1)}, bf16[32,8,128]{2,1,0:T(8,128)(2,1)S(1)}) custom-call(f32[1,2,16,2048]{3,2,1,0:T(8,128)S(1)} %copy-done, bf16[16,32,128]{2,1,0:T(8,128)(2,1)S(1)} %all_to_all.22.refs_1_, bf16[1,8,4,2,32,256]{5,4,3,2,1,0:T(8,128)(2,1)S(1)} %get-tuple-element.12.refs_2_, ...), custom_call_target="tpu_custom_call" | custom-call | flops 67108864 | bytes 2097152 | tf_op jit(solution)/shard_map/adjoint/pallas_call | solution.py:416
  48.5 11.6 %all_to_all.23.refs_1_ = bf16[32,8,128]{2,1,0:T(8,128)(2,1)S(1)} all-to-all(bf16[32,8,128]{2,1,0:T(8,128)(2,1)S(1)} %get-tuple-element.16), channel_id=1, replica_groups={{480,496,448,464,32,48,0,16,96,112,64,80,160,176,128,144,224,240,192,20..., dimensions={0} | all-to-all | bytes 131072 | tf_op jit(solution)/shard_map/all_to_all | solution.py:469
  60.1 1.3 %back.1 = (f32[1,2,16,2048]{3,2,1,0:T(8,128)}, bf16[2,1,256,1024]{3,2,1,0:T(8,128)(2,1)}) custom-call(f32[1,2,16,2048]{3,2,1,0:T(8,128)S(1)} %get-tuple-element.15.refs_0_, bf16[32,8,128]{2,1,0:T(8,128)(2,1)S(1)} %all_to_all.23.refs_1_, bf16[16,1024]{1,0:T(8,128)(2,1)S(1)} %get-tuple-element.17.refs_2_), custom_call_target="tpu_custom_call" | custom-call | flops 16777216 | bytes 1048576 | tf_op jit(solution)/shard_map/back/pallas_call | solution.py:439
  (1 shorter events, 0.0 us)
Async XLA Ops:
  36.3 11.4 %copy-start = (f32[1,2,16,2048]{3,2,1,0:T(8,128)S(1)}, f32[1,2,16,2048]{3,2,1,0:T(8,128)}, u32[]{:S(2)}) copy-start(f32[1,2,16,2048]{3,2,1,0:T(8,128)} %refs_0_.3) | copy-start | bytes 786436

commit v9 on v8

--- a/solution.py
+++ b/solution.py
@@ -46,7 +46,12 @@
 
     chips = col_shards // 2
     columns = [2 * ((chips // 2 + 3 * i) % chips) + core for core in (1, 0) for i in range(chips)]
-    return blocks(row_shards - 1), columns, blocks(row_shards // 2)
+    outward = [
+        f * row_shards + r
+        for r in turned(row_shards, row_shards - 1)
+        for f in turned(freq_shards, freq_shards - 1)
+    ]
+    return outward, columns, blocks(row_shards // 2)
 
 
 def in_hbm(array):

time: 61.7 us -> 61.8 us (level)
  no operation moved by 1% of the time
where the time goes in v9:
time: 61.8 us; the launch traced here: 61.3 us
  blocking collectives  55.9 us (90%)
  Pallas kernels  4.77 us (8%)
  between operations  0.66 us (1%)
    all_to_all x4, blocking collectives, exchange(): lax.all_to_all(chunks, axes, split_axis=0, concat_axis=0, tiled=True, axi...  55.9 us
    pallas_call x1, Pallas kernels, spectrum_chunks(): pl.pallas_call(lambda *refs: spectrum_kernel(1.0 / math.sqrt(trace_len),...  1.93 us
    pallas_call x1, Pallas kernels, back_traces(): pl.pallas_call(lambda *refs: back_kernel(1.0 / math.sqrt(freq_count), ord...  1.27 us

profile of v9, /device:TPU:1, one launch (start us, length us, event | category | flops | bytes accessed | tf_op | source)
XLA Modules:
  0.0 61.3 jit_solution(18176731074758109465)
XLA Ops:
  0.6 1.9 %spectrum.1 = (bf16[32,8,128]{2,1,0:T(8,128)(2,1)S(1)}, bf16[16,1024]{1,0:T(8,128)(2,1)S(1)}, bf16[1,8,4,2,32,256]{5,4,3,2,1,0:T(8,128)(2,1)S(1)}, bf16[1,8,4,2,...) custom-call(bf16[2,1,256,1024]{3,2,1,0:T(8,128)(2,1)} %refs_0_.2, ...), custom_call_target="tpu_custom_call" | custom-call | flops 16777216 | bytes 5242880 | tf_op jit(solution)/shard_map/spectrum/pallas_call | solution.py:360
  2.6 20.3 %all_to_all.20.refs_0_ = bf16[32,8,128]{2,1,0:T(8,128)(2,1)S(1)} all-to-all(bf16[32,8,128]{2,1,0:T(8,128)(2,1)S(1)} %get-tuple-element.10), channel_id=1, replica_groups={{496,48,112,176,240,304,368,432,448,0,64,128,192,256,320,384,464,16,80,..., dimensions={0} | all-to-all | bytes 131072 | tf_op jit(solution)/shard_map/all_to_all | solution.py:474
  22.9 0.7 %forward.1 = bf16[16,32,128]{2,1,0:T(8,128)(2,1)S(1)} custom-call(bf16[32,8,128]{2,1,0:T(8,128)(2,1)S(1)} %all_to_all.20.refs_0_, bf16[1,8,4,2,32,256]{5,4,3,2,1,0:T(8,128)(2,1)S(1)} %get-tuple-element.11.refs_1_.refs_3_, bf16[1,8,4,2,32,256]{5,4,3,2,1,0:T(8,128)(2,1)S(1)} %get-tuple-element.12.refs_2_, f32[4,512]{1,0:T(4,128)S(1)} %get-tuple-element.13.refs_3_), custom_call_target="tpu_custom_call" | custom-call | flops 67108864 | bytes 2097152 | tf_op jit(solution)/shard_map/forward/pallas_call | solution.py:388
  23.6 12.9 %all_to_all.21.refs_0_ = bf16[16,32,128]{2,1,0:T(8,128)(2,1)S(1)} all-to-all(bf16[16,32,128]{2,1,0:T(8,128)(2,1)S(1)} %forward.1), channel_id=1, replica_groups={{9,15,5,11,1,7,13,3,8,14,4,10,0,6,12,2},{25,31,21,27,17,23,29,19,24,30,..., dimensions={0} | all-to-all | bytes 262144 | tf_op jit(solution)/shard_map/all_to_all | solution.py:474
  36.5 0.0 copy-start
  36.5 11.3 %all_to_all.22.refs_1_ = bf16[16,32,128]{2,1,0:T(8,128)(2,1)S(1)} all-to-all(bf16[16,32,128]{2,1,0:T(8,128)(2,1)S(1)} %total.1), channel_id=1, replica_groups={{9,15,5,11,1,7,13,3,8,14,4,10,0,6,12,2},{25,31,21,27,17,23,29,19,24,30,..., dimensions={0} | all-to-all | bytes 262144 | tf_op jit(solution)/shard_map/all_to_all | solution.py:474
  47.8 0.0 copy-done
  47.8 0.8 %adjoint.1 = (f32[1,2,16,2048]{3,2,1,0:T(8,128)S(1)}, bf16[32,8,128]{2,1,0:T(8,128)(2,1)S(1)}) custom-call(f32[1,2,16,2048]{3,2,1,0:T(8,128)S(1)} %copy-done, bf16[16,32,128]{2,1,0:T(8,128)(2,1)S(1)} %all_to_all.22.refs_1_, bf16[1,8,4,2,32,256]{5,4,3,2,1,0:T(8,128)(2,1)S(1)} %get-tuple-element.12.refs_2_, ...), custom_call_target="tpu_custom_call" | custom-call | flops 67108864 | bytes 2097152 | tf_op jit(solution)/shard_map/adjoint/pallas_call | solution.py:421
  48.6 11.4 %all_to_all.23.refs_1_ = bf16[32,8,128]{2,1,0:T(8,128)(2,1)S(1)} all-to-all(bf16[32,8,128]{2,1,0:T(8,128)(2,1)S(1)} %get-tuple-element.16), channel_id=1, replica_groups={{480,496,448,464,32,48,0,16,96,112,64,80,160,176,128,144,224,240,192,20..., dimensions={0} | all-to-all | bytes 131072 | tf_op jit(solution)/shard_map/all_to_all | solution.py:474
  60.1 1.3 %back.1 = (f32[1,2,16,2048]{3,2,1,0:T(8,128)}, bf16[2,1,256,1024]{3,2,1,0:T(8,128)(2,1)}) custom-call(f32[1,2,16,2048]{3,2,1,0:T(8,128)S(1)} %get-tuple-element.15.refs_0_, bf16[32,8,128]{2,1,0:T(8,128)(2,1)S(1)} %all_to_all.23.refs_1_, bf16[16,1024]{1,0:T(8,128)(2,1)S(1)} %get-tuple-element.17.refs_2_), custom_call_target="tpu_custom_call" | custom-call | flops 16777216 | bytes 1048576 | tf_op jit(solution)/shard_map/back/pallas_call | solution.py:444
  (1 shorter events, 0.0 us)
Async XLA Ops:
  36.5 11.4 %copy-start = (f32[1,2,16,2048]{3,2,1,0:T(8,128)S(1)}, f32[1,2,16,2048]{3,2,1,0:T(8,128)}, u32[]{:S(2)}) copy-start(f32[1,2,16,2048]{3,2,1,0:T(8,128)} %refs_0_.3) | copy-start | bytes 786436
